TPU v7x, 256 devices: a whole 4x4x8 slice. The times are simulated.
256 devices in a mesh: sp: 32 (over z, y), cp: 8 (over x, core).
Axes of the slice: x: 4, y: 4, z: 8, core: 2. Of those that a mesh axis runs over, the one named last changes fastest.
Arguments:
- queries: bfloat16 [32768, 4096], P(('cp', 'sp')), may hold values from -80 to 80
- keyvals: bfloat16 [32768, 4, 256], P(('cp', 'sp')), may hold values from -8 to 8
- residual: bfloat16 [32768, 2048], P(('cp', 'sp')), may hold values from -3 to 3
- out_weight: bfloat16 [4096, 2048], P('cp'), may hold values from -0.09375 to 0.09375
- norm_gain: float32 [2048], replicated, may hold values from 0.5 to 2
- doc_ids: int32 [32768], replicated, may hold values from 0 to 63, never falling along the last dimension, each value on 1 to 1024 neighbouring positions
- expert_ids: int32 [32768, 8], P(('cp', 'sp')), may hold values from 0 to 127, all different within a row
- route_weights: float32 [32768, 8], P(('cp', 'sp')), may hold values from 0.05 to 0.5
- expert_in: bfloat16 [256, 2048, 768], P(('sp', 'cp')), may hold values from -0.125 to 0.125
- expert_out: bfloat16 [256, 384, 2048], P(('sp', 'cp')), may hold values from -0.21875 to 0.21875
Outputs:
- mixed: bfloat16 [32768, 2048], P(('cp', 'sp'))
Inputs may be any that keep to these rules, and one draw needn't show every extreme that they name: `doc_ids`: document numbers never fall along the positions, and a document holds at most 1024 positions. `expert_ids`: each token names 8 different experts.
All inputs are finite; a program needn't handle non-finite values.
Results may differ from a plain program's by a relative error of at most 0.022.
Values may be sent and summed in bfloat16 or wider, within the bound.
A program may use at most 128 MiB of HBM per device.

v0:
```python
import math

import jax
import jax.numpy as jnp
from jax import lax
from jax.sharding import PartitionSpec as P

EXP_SP = 4


def from_behind(block, axis, distance):
    devices = range(lax.axis_size(axis))
    route = [(i - distance, i) for i in devices if i - distance in devices]
    return lax.ppermute(block, axis, route)


def on_device(
    queries,
    keyvals,
    residual,
    out_weight,
    norm_gain,
    doc_ids,
    expert_ids,
    route_weights,
    expert_in,
    expert_out,
):
    tok_rows = queries.shape[0]
    sp_count = lax.axis_size("sp")
    cp_count = lax.axis_size("cp")
    head_dim = keyvals.shape[2] // 2
    heads_all = queries.shape[1] // head_dim
    kv_heads = keyvals.shape[1]
    heads_here = heads_all // sp_count
    q_local = queries.reshape(tok_rows, heads_all, head_dim)
    repeated = jnp.repeat(keyvals, heads_all // kv_heads, axis=1)
    q_heads, kv_here = (
        lax.all_to_all(q_local, "sp", split_axis=1, concat_axis=0, tiled=True),
        lax.all_to_all(repeated, "sp", split_axis=1, concat_axis=0, tiled=True),
    )
    block_len = tok_rows * sp_count
    doc_span = block_len // 4
    left_tail = from_behind(kv_here[block_len - doc_span :], "cp", 1)
    key_rows = jnp.concatenate([left_tail, kv_here], axis=0)
    offset = lax.axis_index("cp") * block_len
    padded_docs = jnp.concatenate([jnp.full((doc_span,), -1, jnp.int32), doc_ids], axis=0)
    key_docs = lax.dynamic_slice_in_dim(padded_docs, offset, doc_span + block_len, 0)
    query_docs = lax.dynamic_slice_in_dim(doc_ids, offset, block_len, 0)
    step_rows = min(512, block_len)
    window = doc_span + step_rows
    score_scale = 1.0 / math.sqrt(head_dim)

    def attend(block_num):
        first_row = block_num * step_rows
        q_block = lax.dynamic_slice_in_dim(q_heads, first_row, step_rows, 0)
        k_block = lax.dynamic_slice_in_dim(key_rows, first_row, window, 0)
        q_docs = lax.dynamic_slice_in_dim(query_docs, first_row, step_rows, 0)
        k_docs = lax.dynamic_slice_in_dim(key_docs, first_row, window, 0)
        q_pos = first_row + jnp.arange(step_rows, dtype=jnp.int32)
        k_pos = first_row - doc_span + jnp.arange(window, dtype=jnp.int32)
        allowed = (k_docs[None, :] == q_docs[:, None]) & (k_pos[None, :] <= q_pos[:, None])
        scores = (
            jnp.einsum(
                "bhd,khd->hbk",
                q_block,
                k_block[:, :, :head_dim],
                preferred_element_type=jnp.float32,
            )
            * score_scale
        )
        scores = jnp.where(allowed[None], scores, jnp.float32(-1e30))
        row_max = jnp.max(scores, axis=-1, keepdims=True)
        exponent = jnp.exp(scores - row_max)
        denominator = jnp.sum(exponent, axis=-1)
        weights_bf = exponent.astype(jnp.bfloat16)
        numerator = jnp.einsum(
            "hbk,khd->bhd", weights_bf, k_block[:, :, head_dim:], preferred_element_type=jnp.float32
        )
        return (numerator / jnp.transpose(denominator)[:, :, None]).astype(jnp.bfloat16)

    attended = lax.map(attend, jnp.arange(block_len // step_rows, dtype=jnp.int32))
    attended = attended.reshape(block_len, heads_here, head_dim)
    grouped = lax.all_to_all(
        lax.all_to_all(attended, "sp", split_axis=0, concat_axis=1, tiled=True),
        "cp",
        split_axis=1,
        concat_axis=0,
        tiled=True,
    )
    flat_rows = grouped.reshape(cp_count * tok_rows, -1)
    projected = lax.psum_scatter(
        jnp.dot(flat_rows, out_weight, preferred_element_type=jnp.float32).astype(jnp.bfloat16),
        "cp",
        scatter_dimension=0,
        tiled=True,
    ).astype(jnp.float32)
    summed = residual.astype(jnp.float32) + projected
    normed = (
        summed * lax.rsqrt(jnp.mean(summed * summed, axis=-1, keepdims=True) + 1e-06) * norm_gain
    ).astype(jnp.bfloat16)
    experts = EXP_SP * sp_count
    part_count = cp_count // EXP_SP
    top_count = expert_ids.shape[1]
    capacity = max(2, tok_rows * top_count // experts)
    model_dim = normed.shape[1]
    flat_ids = expert_ids.reshape(-1)
    one_hot = (flat_ids[:, None] == jnp.arange(experts, dtype=jnp.int32)[None, :]).astype(jnp.int32)
    before = jnp.cumsum(one_hot, axis=0, dtype=jnp.int32) - one_hot
    slot_rank = jnp.sum(before * one_hot, axis=1, dtype=jnp.int32)
    kept_mask = slot_rank < capacity
    slot_index = jnp.where(kept_mask, flat_ids * capacity + slot_rank, experts * capacity)
    owners = jnp.arange(tok_rows * top_count, dtype=jnp.int32) // top_count
    slot_table = (
        jnp.full((experts * capacity,), -1, jnp.int32).at[slot_index].set(owners, mode="drop")
    )
    picked = jnp.where(
        (slot_table >= 0)[:, None],
        jnp.take(normed, jnp.maximum(slot_table, 0), axis=0),
        jnp.zeros((), jnp.bfloat16),
    )
    outgoing = jnp.broadcast_to(
        picked.reshape(sp_count, EXP_SP, 1, capacity, model_dim),
        (sp_count, EXP_SP, part_count, capacity, model_dim),
    )
    outgoing = outgoing.reshape(sp_count, cp_count, capacity, model_dim)
    incoming = lax.all_to_all(
        lax.all_to_all(outgoing, "sp", split_axis=0, concat_axis=0, tiled=True),
        "cp",
        split_axis=1,
        concat_axis=1,
        tiled=True,
    )
    rows_in = incoming.reshape(-1, model_dim)
    part_width = expert_out.shape[1]
    gate_up = jnp.dot(rows_in, expert_in[0], preferred_element_type=jnp.float32)
    activated = (jax.nn.silu(gate_up[:, :part_width]) * gate_up[:, part_width:]).astype(
        jnp.bfloat16
    )
    result = jnp.dot(activated, expert_out[0], preferred_element_type=jnp.float32).astype(
        jnp.bfloat16
    )
    result = result.reshape(sp_count, cp_count, capacity, model_dim)
    returned = lax.all_to_all(
        lax.all_to_all(result, "sp", split_axis=0, concat_axis=0, tiled=True),
        "cp",
        split_axis=1,
        concat_axis=1,
        tiled=True,
    )
    merged = jnp.sum(
        returned.reshape(sp_count, EXP_SP, part_count, capacity, model_dim),
        axis=2,
        dtype=jnp.float32,
    ).astype(jnp.bfloat16)
    flat_out = merged.reshape(experts * capacity, model_dim)
    lookup = flat_ids * capacity + jnp.minimum(slot_rank, capacity - 1)
    gathered = jnp.take(flat_out, lookup, axis=0)
    scale_route = jnp.where(kept_mask, route_weights.reshape(-1), jnp.float32(0.0))
    moe_sum = jnp.sum(
        (gathered.astype(jnp.float32) * scale_route[:, None]).reshape(
            tok_rows, top_count, model_dim
        ),
        axis=1,
    )
    return (summed + moe_sum).astype(jnp.bfloat16)


def solution(mesh):
    placed = (
        P(("cp", "sp"), None),
        P(("cp", "sp"), None, None),
        P(("cp", "sp"), None),
        P("cp", None),
        P(),
        P(),
        P(("cp", "sp"), None),
        P(("cp", "sp"), None),
        P(("sp", "cp"), None, None),
        P(("sp", "cp"), None, None),
    )
    return jax.shard_map(
        on_device, mesh=mesh, in_specs=placed, out_specs=P(("cp", "sp"), None), check_vma=False
    )
```

profile of v0, /device:TPU:2, one launch (start us, length us, event | category | flops | bytes accessed | tf_op | source)
XLA Modules:
  0.0 979.4 jit_solution(15885009550596633394)
XLA Ops:
  9.2 11.6 %all-to-all-start = ((bf16[128,32,256]{2,0,1:T(8,128)(2,1)}), bf16[128,32,256]{2,0,1:T(8,128)(2,1)}, u32[]{:S(2)}, u32[]{:S(2)}) async-start(bf16[128,32,256]{2,0,1:T(8,128)(2,1)} %bitcast.102), calls=%async_computation | async-start | bytes 4194304 | tf_op jit(solution)/shard_map/all_to_all | solution.py:40
  23.2 47.8 %all-to-all-done = bf16[128,32,256]{2,0,1:T(8,128)(2,1)} async-done(((bf16[128,32,256]{2,0,1:T(8,128)(2,1)}), bf16[128,32,256]{2,0,1:T(8,128)(2,1)}, u32[]{:S(2)}, u32[]{:S(2)}) %all-to-all-start) | async-done | bytes 2097184 | tf_op jit(solution)/shard_map/all_to_all | solution.py:40
  71.0 6.1 all-to-all-start.1
  80.9 23.1 %all-to-all-done.1 = bf16[128,32,128]{0,2,1:T(8,128)(2,1)} async-done(((bf16[128,32,128]{0,2,1:T(8,128)(2,1)}), bf16[128,32,128]{0,2,1:T(8,128)(2,1)}, u32[]{:S(2)}, u32[]{:S(2)}) %all-to-all-start.1) | async-done | bytes 1048608 | tf_op jit(solution)/shard_map/all_to_all | solution.py:39
  109.7 74.0 %while.12 = (s32[]{:T(128)}, bf16[8,512,1,128]{3,1,0,2:T(8,128)(2,1)}, s32[8]{0:T(128)S(1)}, bf16[5120,1,256]{2,0,1:T(8,128)(2,1)}, s32[5120]{0:T(1024)S(1)}, /*...) while((s32[]{:T(128)}, ...), condition=%wide.region_3.4_spmd, body=%wide.region_0.3_spmd.sunk | while | flops 410649600 | bytes 23644972 | solution.py:82
  189.8 32.3 %all_to_all.89 = bf16[32,2,8192]{2,1,0:T(2,128)(2,1)} all-to-all(bf16[32,2,8192]{2,1,0:T(2,128)(2,1)} %reshape.263), channel_id=1, replica_groups=mesh['sp'=32,'cp'=8] {'sp'}, dimensions={0} | all-to-all | bytes 2097152 | tf_op jit(solution)/shard_map/all_to_all | solution.py:85
  222.0 5.8 reshape.264
  229.5 19.4 %all_to_all.90 = bf16[128,32,128]{2,0,1:T(8,128)(2,1)} all-to-all(bf16[128,32,128]{2,0,1:T(8,128)(2,1)S(1)} %bitcast.103), channel_id=1, replica_groups=mesh['sp'=32,'cp'=8] {'cp'}, dimensions={1} | all-to-all | bytes 2097152 | tf_op jit(solution)/shard_map/all_to_all | solution.py:84
  251.3 6.2 convolution_convert_fusion.1
  268.0 22.8 %reduce-scatter.2.cloned.1.call-done = bf16[128,2048]{1,0:T(8,128)(2,1)} async-done(((bf16[1024,2048]{1,0:T(8,128)(2,1)}), bf16[128,2048]{1,0:T(8,128)(2,1)}) %reduce-scatter.2.cloned.1.call-update) | async-done | bytes 524304 | tf_op jit(solution)/shard_map/reduce_scatter | solution.py:92
  294.5 9.9 %gather_fusion = bf16[1024,2048]{1,0:T(8,128)(2,1)} fusion(bf16[128,2048]{1,0:T(8,128)(2,1)} %multiply_convert_fusion, s32[1024]{0:T(1024)S(1)} %maximum_clamp_fusion), kind=kCustom, calls=%fused_computation | custom fusion | bytes 8392704 | tf_op jit(solution)/shard_map/jit(_take)/gather | solution.py:119
  308.3 6.8 broadcast_in_dim.88
  315.1 195.5 %all_to_all.91 = bf16[32,8,8,2048]{3,2,1,0:T(8,128)(2,1)} all-to-all(bf16[32,8,8,2048]{3,2,1,0:T(8,128)(2,1)} %bitcast.98), channel_id=1, replica_groups=mesh['sp'=32,'cp'=8] {'sp'}, dimensions={0} | all-to-all | bytes 16777216 | tf_op jit(solution)/shard_map/all_to_all | solution.py:128
  510.6 8.3 copy.93
  518.9 101.3 %all_to_all.92 = bf16[32,8,8,2048]{3,2,0,1:T(8,128)(2,1)} all-to-all(bf16[32,8,8,2048]{3,2,0,1:T(8,128)(2,1)} %copy.93), channel_id=1, replica_groups=mesh['sp'=32,'cp'=8] {'cp'}, dimensions={1} | all-to-all | bytes 16777216 | tf_op jit(solution)/shard_map/all_to_all | solution.py:127
  620.2 8.3 copy.94
  628.5 9.1 fusion.23
  642.5 190.3 %all_to_all.93 = bf16[32,8,8,2048]{3,2,1,0:T(8,128)(2,1)} all-to-all(bf16[32,8,8,2048]{3,2,1,0:T(8,128)(2,1)S(1)} %bitcast.101), channel_id=1, replica_groups=mesh['sp'=32,'cp'=8] {'sp'}, dimensions={0} | all-to-all | bytes 16777216 | tf_op jit(solution)/shard_map/all_to_all | solution.py:145
  832.8 8.3 copy.95
  841.0 6.4 all-to-all-start.7
  848.0 92.7 %all-to-all-done.7 = bf16[32,8,8,2048]{3,2,0,1:T(8,128)(2,1)} async-done(((bf16[32,8,8,2048]{3,2,0,1:T(8,128)(2,1)}), bf16[32,8,8,2048]{3,2,0,1:T(8,128)(2,1)}, u32[]{:S(2)}, u32[]{:S(2)}) %all-to-all-start.7) | async-done | bytes 8388640 | tf_op jit(solution)/shard_map/all_to_all | solution.py:144
  940.7 8.8 bitcast_reduce_fusion
  954.2 11.7 %gather_fusion.1 = bf16[1024,2048]{1,0:T(8,128)(2,1)} fusion(bf16[1024,2048]{1,0:T(8,128)(2,1)} %bitcast.97, s32[1024]{0:T(1024)S(1)} %broadcast_clamp_fusion), kind=kCustom, calls=%fused_computation.1 | custom fusion | bytes 8392704 | tf_op jit(solution)/shard_map/jit(_take)/gather | solution.py:158
  965.9 5.7 multiply_reduce_fusion
  (174 shorter events, 122.1 us)
Async XLA Ops:
  6.5 621.9 %copy-start = (bf16[1,2048,768]{2,1,0:T(8,128)(2,1)S(1)}, bf16[1,2048,768]{2,1,0:T(8,128)(2,1)}, u32[]{:S(2)}) copy-start(bf16[1,2048,768]{2,1,0:T(8,128)(2,1)} %param.20) | copy-start | bytes 9437188
  9.2 61.8 %all-to-all-start = ((bf16[128,32,256]{2,0,1:T(8,128)(2,1)}), bf16[128,32,256]{2,0,1:T(8,128)(2,1)}, u32[]{:S(2)}, u32[]{:S(2)}) async-start(bf16[128,32,256]{2,0,1:T(8,128)(2,1)} %bitcast.102), calls=%async_computation | async-start | bytes 4194304 | tf_op jit(solution)/shard_map/all_to_all | solution.py:40
  20.8 60.1 %copy-start.6 = (s32[32768]{0:T(1024)S(1)}, s32[32768]{0:T(1024)}, u32[]{:S(2)}) copy-start(s32[32768]{0:T(1024)} %param.17) | copy-start | bytes 393220
  71.0 33.1 %all-to-all-start.1 = ((bf16[128,32,128]{0,2,1:T(8,128)(2,1)}), bf16[128,32,128]{0,2,1:T(8,128)(2,1)}, u32[]{:S(2)}, u32[]{:S(2)}) async-start(bf16[128,32,128]{0,2,1:T(8,128)(2,1)} %bitcast.104), calls=%async_computation.1 | async-start | bytes 2097152 | tf_op jit(solution)/shard_map/all_to_all | solution.py:39
  77.0 213.8 %reduce-scatter.2.cloned.1.call-start = ((), (), s32[]{:S(2)}) async-start(), calls=%async_computation.9 | async-start | bytes 4718592 | tf_op jit(solution)/shard_map/reduce_scatter | solution.py:92
  79.0 27.4 %collective-permute-start = (bf16[1024,1,256]{2,0,1:T(8,128)(2,1)}, bf16[1024,1,256]{2,0,1:T(8,128)(2,1)}, u32[]{:S(2)}, u32[]{:S(2)}) collective-permute-start(bf16[1024,1,256]{2,0,1:T(8,128)(2,1)} %bitcast.10), channel_id=1, source_target_pairs={{0,1},{1,2},{2,3},{3,4},{4,5},{5,6},{6,7},{8,9},{9,10},{10,11},{11... | collective-permute-start | bytes 1572872 | tf_op jit(solution)/shard_map/ppermute | solution.py:14
  106.3 3.4 dynamic-slice-start
  113.2 1.7 copy-start.2
  122.4 1.7 copy-start.2
  131.7 1.7 copy-start.2
  140.9 1.7 copy-start.2
  150.2 1.7 copy-start.2
  159.4 1.7 copy-start.2
  168.7 1.7 copy-start.2
  177.9 1.7 copy-start.2
  257.6 0.7 copy-start.7
  258.2 34.1 %copy-start.8 = (f32[2048]{0:T(1024)S(1)}, f32[2048]{0:T(1024)}, u32[]{:S(2)}) copy-start(f32[2048]{0:T(1024)} %param.16) | copy-start | bytes 24580
  258.8 0.8 copy-start.5
  628.5 9.2 copy-start.10
  841.0 6.5 copy-start.9
  841.0 99.7 %all-to-all-start.7 = ((bf16[32,8,8,2048]{3,2,0,1:T(8,128)(2,1)}), bf16[32,8,8,2048]{3,2,0,1:T(8,128)(2,1)}, u32[]{:S(2)}, u32[]{:S(2)}) async-start(bf16[32,8,8,2048]{3,2,0,1:T(8,128)(2,1)} %copy.95), calls=%async_computation.8 | async-start | bytes 16777216 | tf_op jit(solution)/shard_map/all_to_all | solution.py:144
  954.2 18.4 %copy-start.1 = (bf16[1,2048,768]{2,1,0:T(8,128)(2,1)S(1)}, bf16[1,2048,768]{2,1,0:T(8,128)(2,1)}, u32[]{:S(2)}) copy-start(bf16[1,2048,768]{2,1,0:T(8,128)(2,1)} %param.20) | copy-start | bytes 9437188
  965.9 5.7 copy-start.3
  965.9 5.7 copy-start.4
Sparse Core Ops, SparseCore 0:
  257.7 33.0 reduce-scatter.1
where the time goes:
time: 983 us; the launch traced here: 979 us
  blocking collectives  539 us (55%)
  waiting for transfers between devices  187 us (19%)
  local copies, waits for them, and re-layouts  113 us (11%)
  matrix products  58.7 us (6%)
  other arithmetic  37 us (4%)
  starting transfers between devices  26.1 us (3%)
  between operations  13.7 us (1%)
    all_to_all x1, blocking collectives, on_device(): lax.all_to_all(outgoing, 'sp', split_axis=0, concat_axis=0, tiled=True)  196 us
    all_to_all x1, blocking collectives, on_device(): lax.all_to_all(result, 'sp', split_axis=0, concat_axis=0, tiled=True)  190 us
    all_to_all x1, blocking collectives, on_device(): lax.all_to_all(lax.all_to_all(outgoing, 'sp', split_axis=0, concat_axis=0...  101 us
    all_to_all x1, waiting for transfers between devices, on_device(): lax.all_to_all(lax.all_to_all(result, 'sp', split_axis=0, concat_axis=0,...  92.7 us
    all_to_all x1, waiting for transfers between devices, on_device(): lax.all_to_all(repeated, 'sp', split_axis=1, concat_axis=0, tiled=True)  47.8 us
    all_to_all x1, blocking collectives, on_device(): lax.all_to_all(attended, 'sp', split_axis=0, concat_axis=1, tiled=True)  32.3 us
    all_to_all x1, waiting for transfers between devices, on_device(): lax.all_to_all(q_local, 'sp', split_axis=1, concat_axis=0, tiled=True)  23.1 us
    reduce_scatter x1, waiting for transfers between devices, on_device(): lax.psum_scatter(jnp.dot(flat_rows, out_weight, preferred_element_type=jn...  22.8 us
  transfers between devices with their start and end apart: 5, of which 4 were waited for; matrix products, arithmetic and copies ran while one was open for 2% of the time, Pallas kernels for 0%

commit v1 on v0

v1 whole, which is shorter than its diff:
```python
import math

import jax
import jax.numpy as jnp
from jax import lax
from jax.experimental import pallas as pl
from jax.experimental.pallas import tpu as pltpu
from jax.sharding import Mesh, PartitionSpec as P

NZ, NY, NX, NC = 8, 4, 4, 2
TOK = 128
HD = 128
KVH = 4
HEADS = 32
GROUP = HEADS // KVH
HG = 4
CAP = 8
DOC_MAX = 1024
SPAN = DOC_MAX + TOK
MESH_AXES = ("z", "y", "x", "c")
COUNT = NZ * NY * NX * NC
PLANE = NY * NX
BLOCK_ORDER = (0, 4, 1, 7, 2, 6, 3, 5)
MESH = pl.DeviceIdType.MESH


def place_of(block):
    sp, cp = block % (NZ * NY), block // (NZ * NY)
    return sp * NX * NC + cp


def from_behind(block, distance):
    route = [(place_of(i), place_of((i + distance) % COUNT)) for i in range(COUNT)]
    return lax.ppermute(block, MESH_AXES, route)


def attention_kernel(q_ref, kv_ref, bias_ref, out_ref, k_ref, v_ref):
    first = lax.axis_index("y")
    scale = math.log2(math.e) / math.sqrt(HD)
    for g in range(KVH):
        for b in range(SPAN // TOK):
            block = first + b
            rows = kv_ref[lax.rem(block, NY), block // NY]
            k_ref[b * TOK : (b + 1) * TOK, :] = rows[:, g * 2 * HD : g * 2 * HD + HD]
            v_ref[b * TOK : (b + 1) * TOK, :] = rows[:, g * 2 * HD + HD : (g + 1) * 2 * HD]

        for i in range(GROUP):
            head = g * GROUP + i
            q = q_ref[:, head * HD : (head + 1) * HD]
            scores = lax.dot_general(
                q, k_ref[...], (((1,), (1,)), ((), ())), preferred_element_type=jnp.float32
            )
            scores = scores * scale + bias_ref[...]
            top = jnp.max(scores, axis=-1, keepdims=True)
            exponent = jnp.exp2(scores - top)
            denominator = jnp.sum(exponent, axis=-1, keepdims=True)
            numerator = jnp.dot(
                exponent.astype(jnp.bfloat16), v_ref[...], preferred_element_type=jnp.float32
            )
            group, inner = head // HG, head % HG
            place = ((group % NC) * NX + group // NC) * HG + inner
            out_ref[:, place * HD : (place + 1) * HD] = (numerator / denominator).astype(
                jnp.bfloat16
            )


def attention(queries, kv_window, bias):
    return pl.pallas_call(
        attention_kernel,
        out_shape=jax.ShapeDtypeStruct(queries.shape, jnp.bfloat16),
        in_specs=[pl.BlockSpec(memory_space=pltpu.VMEM)] * 3,
        out_specs=pl.BlockSpec(memory_space=pltpu.VMEM),
        scratch_shapes=[
            pltpu.VMEM((SPAN, HD), jnp.bfloat16),
            pltpu.VMEM((SPAN, HD), jnp.bfloat16),
        ],
        compiler_params=pltpu.CompilerParams(vmem_limit_bytes=40 * 2**20),
        cost_estimate=pl.CostEstimate(
            flops=4 * HEADS * TOK * SPAN * HD, bytes_accessed=8 * 2**20, transcendentals=HEADS * TOK * SPAN
        ),
        name="attention",
    )(queries, kv_window, bias)


def moe_kernel(
    normed_ref,
    summed_ref,
    pick_ref,
    spread_ref,
    w_in_hbm,
    w_out_hbm,
    out_ref,
    col,
    stage,
    recv,
    result,
    back,
    acc,
    ring,
    home,
    w_in,
    w_out,
    own_sem,
    w_send,
    w_recv,
    col_send,
    col_recv,
    out_send,
    out_recv,
    back_send,
    back_recv,
    ring_send,
    ring_recv,
):
    z, y, x, c = (lax.axis_index(name) for name in MESH_AXES)
    right, left = lax.rem(z + 1, NZ), lax.rem(z + NZ - 1, NZ)
    place = y * NX + x
    model = normed_ref.shape[1]
    step = 512
    half = TOK // 2

    def peer(k):
        other_y, other_x = lax.rem(y + k // NX, NY), lax.rem(x + k % NX, NX)
        return {"y": other_y, "x": other_x}, other_y * NX + other_x

    barrier = pltpu.get_barrier_semaphore()

    def greet(k, carry):
        pl.semaphore_signal(barrier, inc=1, device_id=peer(k)[0], device_id_type=MESH)
        return carry

    lax.fori_loop(1, PLANE, greet, 0)
    for other in ({"z": right}, {"z": left}, {"c": 1 - c}):
        pl.semaphore_signal(barrier, inc=1, device_id=other, device_id_type=MESH)
    pl.semaphore_wait(barrier, PLANE - 1 + 3)

    def ring_copy(direction, number):
        source = number - 1 if direction == 0 else (NZ + 1 - number) % NZ
        target = number if direction == 0 else NZ - number
        rows = (0, TOK) if number < 4 else ((0, half) if direction == 0 else (half, half))

        def view(block):
            pair, side = (block, 0) if block < 4 else ((NZ - block) % 4, 1)
            return col.at[pair, pl.ds(side * TOK + rows[0], rows[1])]

        return pltpu.make_async_remote_copy(
            src_ref=view(source),
            dst_ref=view(target),
            send_sem=col_send.at[direction, number - 1],
            recv_sem=col_recv.at[direction, number - 1],
            device_id={"z": right if direction == 0 else left},
            device_id_type=MESH,
        )

    col[0, 0:TOK, :] = normed_ref[...]
    for direction in range(2):
        ring_copy(direction, 1).start()

    weight_copies = []
    for n, (hbm, vmem) in enumerate(((w_in_hbm, w_in), (w_out_hbm, w_out))):
        own = pltpu.make_async_copy(hbm.at[0], vmem.at[c], own_sem.at[n])
        given = pltpu.make_async_remote_copy(
            src_ref=hbm.at[0],
            dst_ref=vmem.at[c],
            send_sem=w_send.at[n],
            recv_sem=w_recv.at[n],
            device_id={"c": 1 - c},
            device_id_type=MESH,
        )
        own.start()
        given.start()
        weight_copies += [own, given]

    def exchange(source, target, sends, recvs, pair):
        def send(k, carry):
            device, expert = peer(k)
            pltpu.make_async_remote_copy(
                src_ref=source.at[pair, expert],
                dst_ref=target.at[pair, place],
                send_sem=sends.at[pair],
                recv_sem=recvs.at[pair],
                device_id=device,
                device_id_type=MESH,
            ).start()
            return carry

        lax.fori_loop(1, PLANE, send, 0)
        target[pair, place] = source[pair, place]

    def whole(source, target, sends, recvs, pair):
        return pltpu.make_async_remote_copy(
            src_ref=source.at[pair, pl.ds(0, PLANE - 1)],
            dst_ref=target.at[pair, pl.ds(0, PLANE - 1)],
            send_sem=sends.at[pair],
            recv_sem=recvs.at[pair],
            device_id={"y": y, "x": x},
            device_id_type=MESH,
        )

    for number in range(1, 5):
        pair = number % 4
        for direction in range(2):
            ring_copy(direction, number).wait_recv()
            if number < 4:
                ring_copy(direction, number + 1).start()

        def select(n, carry, pair=pair):
            columns = pl.ds(pl.multiple_of(n * step, step), step)
            rows = jnp.dot(
                pick_ref[pair], col[pair, :, columns], preferred_element_type=jnp.float32
            )
            stage[pair, :, :, columns] = rows.astype(jnp.bfloat16).reshape(PLANE, 2 * CAP, step)
            return carry

        lax.fori_loop(0, model // step, select, 0)
        exchange(stage, recv, out_send, out_recv, pair)

    for copy in weight_copies:
        copy.wait()

    def expert(pair):
        whole(stage, recv, out_send, out_recv, pair).wait_recv()
        rows = recv[pair].reshape(PLANE * 2 * CAP, model)
        width = w_out.shape[1]
        acts = []
        for p in range(2):
            gate_up = jnp.dot(rows, w_in[p], preferred_element_type=jnp.float32)
            gate, up = gate_up[:, :width], gate_up[:, width:]
            acts.append((gate / (1.0 + jnp.exp(-gate)) * up).astype(jnp.bfloat16))

        def down(n, carry):
            columns = pl.ds(pl.multiple_of(n * step, step), step)
            total = jnp.dot(acts[0], w_out[0, :, columns], preferred_element_type=jnp.float32)
            total += jnp.dot(acts[1], w_out[1, :, columns], preferred_element_type=jnp.float32)
            result[pair, :, :, columns] = total.astype(jnp.bfloat16).reshape(
                PLANE, 2 * CAP, step
            )
            return carry

        lax.fori_loop(0, model // step, down, 0)

    def early(n, carry):
        expert(n + 1)
        return carry

    lax.fori_loop(0, 3, early, 0)
    exchange(result, back, back_send, back_recv, 3)
    expert(0)
    for pair in (0, 2, 1):
        exchange(result, back, back_send, back_recv, pair)

    def sum_copy(direction, pair):
        if pair == 0:
            source = acc.at[0, pl.ds(TOK + direction * half, half)]
            target = ring.at[3, pl.ds(direction * (TOK + half), half)]
        else:
            source = acc.at[pair, pl.ds(direction * TOK, TOK)]
            target = ring.at[pair - 1, pl.ds(direction * TOK, TOK)]
        return pltpu.make_async_remote_copy(
            src_ref=source,
            dst_ref=target,
            send_sem=ring_send.at[direction, pair],
            recv_sem=ring_recv.at[direction, pair],
            device_id={"z": left if direction == 0 else right},
            device_id_type=MESH,
        )

    for pair in (0, 3, 2, 1):
        whole(result, back, back_send, back_recv, pair).wait_recv()
        if pair > 0:
            for direction in range(2):
                sum_copy(direction, (pair + 1) % 4).wait_recv()

        def weigh(n, carry, pair=pair):
            columns = pl.ds(pl.multiple_of(n * step, step), step)
            rows = back[pair, :, :, columns].reshape(PLANE * 2 * CAP, step)
            total = jnp.zeros((2 * TOK, step), jnp.float32)
            for part in range(2):
                total += lax.dot_general(
                    spread_ref[part, pair],
                    rows,
                    (((0,), (0,)), ((), ())),
                    preferred_element_type=jnp.float32,
                )
            if pair == 0:
                home[:, columns] = total[:TOK]
                acc[0, TOK:, columns] = total[TOK:].astype(jnp.bfloat16)
            elif pair == 3:
                low = ring[3, 0:half, columns].astype(jnp.float32)
                high = ring[3, TOK + half :, columns].astype(jnp.float32)
                acc[3, 0:half, columns] = (total[:half] + low).astype(jnp.bfloat16)
                acc[3, half : TOK + half, columns] = total[half : TOK + half].astype(jnp.bfloat16)
                acc[3, TOK + half :, columns] = (total[TOK + half :] + high).astype(jnp.bfloat16)
            else:
                came = ring[pair, :, columns].astype(jnp.float32)
                acc[pair, :, columns] = (total + came).astype(jnp.bfloat16)
            return carry

        lax.fori_loop(0, model // step, weigh, 0)
        for direction in range(2):
            sum_copy(direction, pair).start()

    for direction in range(2):
        sum_copy(direction, 1).wait_recv()

    def finish(n, carry):
        columns = pl.ds(pl.multiple_of(n * step, step), step)
        moe_sum = home[:, columns]
        moe_sum += ring[0, 0:TOK, columns].astype(jnp.float32)
        moe_sum += ring[0, TOK:, columns].astype(jnp.float32)
        out_ref[:, columns] = (summed_ref[:, columns] + moe_sum).astype(jnp.bfloat16)
        return carry

    lax.fori_loop(0, model // step, finish, 0)

    for pair in range(4):
        whole(stage, recv, out_send, out_recv, pair).wait_send()
        whole(result, back, back_send, back_recv, pair).wait_send()
        for direction in range(2):
            ring_copy(direction, pair + 1).wait_send()
            sum_copy(direction, pair).wait_send()


def moe(normed, summed, pick, spread, expert_in, expert_out):
    model = normed.shape[1]
    vmem, hbm = pl.BlockSpec(memory_space=pltpu.VMEM), pl.BlockSpec(memory_space=pl.ANY)
    slots = (4, PLANE, 2 * CAP, model)
    blocks = (4, 2 * TOK, model)
    dma = pltpu.SemaphoreType.DMA
    return pl.pallas_call(
        moe_kernel,
        out_shape=jax.ShapeDtypeStruct(normed.shape, jnp.bfloat16),
        in_specs=[vmem] * 4 + [hbm] * 2,
        out_specs=vmem,
        scratch_shapes=[
            pltpu.VMEM(blocks, jnp.bfloat16),
            pltpu.VMEM(slots, jnp.bfloat16),
            pltpu.VMEM(slots, jnp.bfloat16),
            pltpu.VMEM(slots, jnp.bfloat16),
            pltpu.VMEM(slots, jnp.bfloat16),
            pltpu.VMEM(blocks, jnp.bfloat16),
            pltpu.VMEM(blocks, jnp.bfloat16),
            pltpu.VMEM((TOK, model), jnp.float32),
            pltpu.VMEM((2,) + expert_in.shape[1:], jnp.bfloat16),
            pltpu.VMEM((2,) + expert_out.shape[1:], jnp.bfloat16),
            dma((2,)),
            dma((2,)),
            dma((2,)),
            dma((2, 4)),
            dma((2, 4)),
            dma((4,)),
            dma((4,)),
            dma((4,)),
            dma((4,)),
            dma((2, 4)),
            dma((2, 4)),
        ],
        compiler_params=pltpu.CompilerParams(
            collective_id=1, has_side_effects=True, vmem_limit_bytes=58 * 2**20
        ),
        cost_estimate=pl.CostEstimate(
            flops=10 * 10**9, bytes_accessed=12 * 2**20, transcendentals=0
        ),
        name="moe",
    )(normed, summed, pick, spread, expert_in, expert_out)


def on_device(
    queries,
    keyvals,
    residual,
    out_weight,
    norm_gain,
    doc_ids,
    expert_ids,
    route_weights,
    expert_in,
    expert_out,
):
    model = residual.shape[1]
    z, y = lax.axis_index("z"), lax.axis_index("y")
    number = ((lax.axis_index("x") * NC + lax.axis_index("c")) * NZ + z) * NY + y

    kv = keyvals.reshape(TOK, -1)
    back1 = from_behind(kv, NY)
    back2 = from_behind(back1, NY)
    kv_window = lax.all_gather(jnp.stack([back2, back1, kv]), "y")

    weight = lax.all_gather(out_weight, "x")
    weight = lax.all_gather(weight, "c").reshape(-1, model)

    routes = jnp.concatenate([expert_ids.astype(jnp.float32), route_weights], axis=1)
    routes = lax.all_gather(routes, "z")
    routes = jnp.take(routes, lax.rem(z + NZ - jnp.array(BLOCK_ORDER), NZ), axis=0)
    ids = routes[:, :, :8].astype(jnp.int32)
    plane_experts = z * PLANE + jnp.arange(PLANE, dtype=jnp.int32)
    hit = ids[:, :, :, None] == plane_experts
    chosen = jnp.any(hit, axis=2)
    weight_of = jnp.sum(jnp.where(hit, routes[:, :, 8:, None], 0.0), axis=2)
    earlier = jnp.tril(jnp.ones((TOK, TOK), jnp.bfloat16), -1)
    rank = jnp.einsum(
        "ts,bse->bte", earlier, chosen.astype(jnp.bfloat16), preferred_element_type=jnp.float32
    ).astype(jnp.int32)
    slot = jnp.where(chosen, rank, CAP)

    def by_expert(values):
        values = values.reshape(4, 2, TOK, PLANE).transpose(0, 3, 1, 2)
        return values.reshape(4, PLANE, 1, 1, 2 * TOK)

    row = jnp.arange(2 * CAP, dtype=jnp.int32)[:, None]
    side = jnp.arange(2 * TOK, dtype=jnp.int32)[None, :] // TOK
    taken = (by_expert(slot)[:, :, 0] == row % CAP) & (row // CAP == side)
    pick = taken.astype(jnp.bfloat16).reshape(4, 2 * TOK, 2 * TOK)
    spread = jnp.where(taken, by_expert(weight_of)[:, :, 0], 0.0).reshape(4, 2 * TOK, 2 * TOK)
    spread_high = lax.reduce_precision(spread, 8, 7)
    spread = jnp.stack([spread_high, spread - spread_high]).astype(jnp.bfloat16)

    padded = jnp.concatenate([jnp.full((DOC_MAX,), -1, jnp.int32), doc_ids], axis=0)
    key_docs = lax.dynamic_slice_in_dim(padded, number * TOK, SPAN, 0)
    query_docs = key_docs[DOC_MAX:]
    allowed = (key_docs[None, :] == query_docs[:, None]) & (
        jnp.arange(SPAN)[None, :] <= jnp.arange(TOK)[:, None] + DOC_MAX
    )
    bias = jnp.where(allowed, 0.0, -1e30).astype(jnp.float32)
    attended = attention(queries, kv_window, bias)

    summed = residual.astype(jnp.float32) + jnp.dot(
        attended, weight, preferred_element_type=jnp.float32
    )
    normed = (
        summed * lax.rsqrt(jnp.mean(summed * summed, axis=-1, keepdims=True) + 1e-06) * norm_gain
    ).astype(jnp.bfloat16)

    return moe(normed, summed, pick, spread, expert_in, expert_out)


def solution(mesh):
    torus = Mesh(mesh.devices.reshape(NZ, NY, NX, NC), ("z", "y", "x", "c"))
    tokens = ("x", "c", "z", "y")
    experts = ("z", "y", "x", "c")
    placed = (
        P(tokens, None),
        P(tokens, None, None),
        P(tokens, None),
        P(("x", "c"), None),
        P(),
        P(),
        P(tokens, None),
        P(tokens, None),
        P(experts, None, None),
        P(experts, None, None),
    )
    return jax.shard_map(
        on_device, mesh=torus, in_specs=placed, out_specs=P(tokens, None), check_vma=False
    )
```

time: 983 us -> 351 us (0.36)
  blocking collectives: 539 us -> 26.1 us
  Pallas kernels: 0 us -> 164 us
  local copies, waits for them, and re-layouts: 113 us -> 6.97 us
  waiting for transfers between devices: 187 us -> 122 us
  matrix products: 58.7 us -> 8.48 us
  other arithmetic: 37 us -> 5.36 us
  starting transfers between devices: 26.1 us -> 2.11 us
    all_to_all x5 -> x0, blocking collectives: 539 us -> none  [the longest x1 196 us: on_device(): lax.all_to_all(outgoing, 'sp', split_axis=0, concat_axis=0, tiled=True)]
    pallas_call x0 -> x2, Pallas kernels: none -> 164 us  [the longest x1 151 us: moe(): pl.pallas_call(moe_kernel, out_shape=jax.ShapeDtypeStruct(normed.shape, j...]
    all_to_all x3 -> x0, waiting for transfers between devices: 164 us -> none  [the longest x1 92.7 us: on_device(): lax.all_to_all(lax.all_to_all(result, 'sp', split_axis=0, concat_axis=0,...]
    all_gather x0 -> x3, waiting for transfers between devices: none -> 103 us  [the longest x1 66.5 us: on_device(): weight = lax.all_gather(out_weight, 'x')]
    dot_general x19 -> x2, matrix products: 58.7 us -> 8.48 us  [the longest x1 8.25 us: on_device(): jnp.dot(attended, weight, preferred_element_type=jnp.float32)]
    all_to_all x5 -> x0, local copies, waits for them, and re-layouts: 29.5 us -> none  [the longest x1 8.27 us: on_device(): lax.all_to_all(outgoing, 'sp', split_axis=0, concat_axis=0, tiled=True)]
    all_gather x0 -> x1, blocking collectives: none -> 26.1 us  [on_device(): routes = lax.all_gather(routes, 'z')]
    all_to_all x3 -> x0, starting transfers between devices: 24.1 us -> none  [the longest x1 11.6 us: on_device(): lax.all_to_all(repeated, 'sp', split_axis=1, concat_axis=0, tiled=True)]
  transfers between devices with their start and end apart: 5 -> 5, of which waited for: 4 -> 5; matrix products, arithmetic and copies ran while one was open for 2% -> 2% of each run, Pallas kernels for 0% -> 4%
where the time goes in v1:
time: 351 us; the launch traced here: 349 us
  Pallas kernels  164 us (47%)
  waiting for transfers between devices  122 us (35%)
  blocking collectives  26.1 us (7%)
  between operations  13.4 us (4%)
  matrix products  8.48 us (2%)
  local copies, waits for them, and re-layouts  6.97 us (2%)
  other arithmetic  5.36 us (2%)
    pallas_call x1, Pallas kernels, moe(): pl.pallas_call(moe_kernel, out_shape=jax.ShapeDtypeStruct(normed.shape, j...  151 us
    all_gather x1, waiting for transfers between devices, on_device(): weight = lax.all_gather(out_weight, 'x')  66.5 us
    all_gather x1, blocking collectives, on_device(): routes = lax.all_gather(routes, 'z')  26.1 us
    all_gather x1, waiting for transfers between devices, on_device(): weight = lax.all_gather(weight, 'c').reshape(-1, model)  22.3 us
    ppermute x2, waiting for transfers between devices, from_behind(): return lax.ppermute(block, MESH_AXES, route)  18.8 us
    all_gather x1, waiting for transfers between devices, on_device(): kv_window = lax.all_gather(jnp.stack([back2, back1, kv]), 'y')  14.2 us
    pallas_call x1, Pallas kernels, attention(): pl.pallas_call(attention_kernel, out_shape=jax.ShapeDtypeStruct(queries.s...  13.3 us
    dot_general x1, matrix products, on_device(): jnp.dot(attended, weight, preferred_element_type=jnp.float32)  8.25 us
  transfers between devices with their start and end apart: 5, of which 5 were waited for; matrix products, arithmetic and copies ran while one was open for 2% of the time, Pallas kernels for 4%

profile of v1, /device:TPU:2, one launch (start us, length us, event | category | flops | bytes accessed | tf_op | source)
XLA Modules:
  0.0 348.7 jit_solution(11473124982595774047)
XLA Ops:
  6.6 0.7 all-gather.10.cloned.1.call-update
  7.3 1.0 copy.32
  8.3 2.0 collective-permute-start
  10.3 9.4 %collective-permute-done = bf16[128,1024]{1,0:T(8,128)(2,1)S(1)} collective-permute-done((bf16[128,1024]{1,0:T(8,128)(2,1)S(1)}, bf16[128,1024]{1,0:T(8,128)(2,1)S(1)}, u32[]{:S(2)}, u32[]{:S(2)}) %collective-permute-start) | collective-permute-done | bytes 262176 | tf_op jit(solution)/shard_map/ppermute | solution.py:34
  19.7 1.1 stack_reshape.3
  20.8 9.4 %collective-permute-done.1 = bf16[128,1024]{1,0:T(8,128)(2,1)S(1)} collective-permute-done((bf16[128,1024]{1,0:T(8,128)(2,1)S(1)}, bf16[128,1024]{1,0:T(8,128)(2,1)S(1)}, u32[]{:S(2)}, u32[]{:S(2)}) %collective-permute-start.1) | collective-permute-done | bytes 262176 | tf_op jit(solution)/shard_map/ppermute | solution.py:34
  30.2 1.0 pad_maximum_fusion.1
  31.3 66.5 %all-gather.10.cloned.1.call-done = bf16[2048,2048]{1,0:T(8,128)(2,1)} async-done(((bf16[512,2048]{1,0:T(8,128)(2,1)}), bf16[2048,2048]{1,0:T(8,128)(2,1)}) %all-gather.10.cloned.1.call-update) | async-done | bytes 8388624 | tf_op jit(solution)/shard_map/all_gather | solution.py:389
  98.0 26.1 %all-gather.3 = f32[1024,16]{0,1:T(8,128)S(1)} all-gather(f32[128,16]{0,1:T(8,128)S(1)} %pad_maximum_fusion.2), channel_id=5, replica_groups=mesh['z'=8,'y'=4,'x'=4,'c'=2] {'z'}, dimensions={0}, use_global_device_ids=true | all-gather | bytes 73728 | tf_op jit(solution)/shard_map/all_gather | solution.py:393
  124.2 0.6 gather_fusion
  125.0 0.1 compare_reduce_fusion
  125.1 0.2 fusion.1
  125.6 1.0 fusion.4.pick_ref
  126.9 0.3 reduce-precision_convert_fusion
  127.3 1.1 pad_maximum_fusion.spread_ref
  128.4 0.2 fusion.6.bias_ref
  128.6 14.2 %all-gather.8.cloned.1.call-done = bf16[12,128,1024]{2,1,0:T(8,128)(2,1)} async-done(((bf16[3,128,1024]{2,1,0:T(8,128)(2,1)}), bf16[12,128,1024]{2,1,0:T(8,128)(2,1)}) %all-gather.8.cloned.1.call-update) | async-done | bytes 3145744 | tf_op jit(solution)/shard_map/all_gather | solution.py:387
  142.8 1.9 copy-done
  144.7 13.3 %attention.1 = bf16[128,4096]{1,0:T(8,128)(2,1)S(1)} custom-call(bf16[128,4096]{1,0:T(8,128)(2,1)S(1)} %copy-done.1, bf16[4,3,128,1024]{3,2,1,0:T(8,128)(2,1)S(1)} %bitcast.42, f32[128,1152]{1,0:T(8,128)S(1)} %fusion.6.bias_ref), custom_call_target="tpu_custom_call" | custom-call | flops 2415919104 | bytes 8388608 | tf_op jit(solution)/shard_map/attention/pallas_call | solution.py:68
  158.0 22.3 %all-gather.12.cloned.1.call-done = bf16[8,512,2048]{2,1,0:T(8,128)(2,1)} async-done(((bf16[4,512,2048]{2,1,0:T(8,128)(2,1)}), bf16[8,512,2048]{2,1,0:T(8,128)(2,1)}) %all-gather.12.cloned.1.call-update) | async-done | bytes 16777232 | tf_op jit(solution)/shard_map/all_gather | solution.py:390
  180.2 8.3 %multiply_reduce_fusion = (f32[128]{0:T(128)S(1)}, f32[128,2048]{1,0:T(8,128)S(1)}) fusion(bf16[128,4096]{1,0:T(8,128)(2,1)S(1)} %attention.1, bf16[4096,2048]{1,0:T(8,128)(2,1)} %bitcast.43, bf16[128,2048]{1,0:T(8,128)(2,1)S(1)} %copy-done.3), kind=kOutput, calls=%fused_computation.11 | convolution fusion | flops 2148532224 | bytes 19399168 | tf_op jit(solution)/shard_map/dot_general | solution.py:427
  188.5 1.1 multiply_convert_fusion.normed_ref
  189.7 150.6 %moe.1 = bf16[128,2048]{1,0:T(8,128)(2,1)} custom-call(bf16[128,2048]{1,0:T(8,128)(2,1)} %multiply_convert_fusion.normed_ref, f32[128,2048]{1,0:T(8,128)} %copy-done.2, bf16[4,256,256]{2,1,0:T(8,128)(2,1)} %fusion.4.pick_ref, bf16[2,4,256,256]{3,2,1,0:T(8,128)(2,1)} %pad_maximum_fusion.spread_ref, bf16[1,2048,768]{2,1,0:T(8,128)(2,1)} %w_in_hbm.1, ...), custom_call_target="tpu_custom_call" | custom-call | flops 10000000000 | bytes 12582912 | tf_op jit(solution)/shard_map/moe/pallas_call | solution.py:330
  340.3 1.9 copy.39
  (48 shorter events, 1.1 us)
Async XLA Ops:
  6.5 117.6 %copy-start.8 = (s32[8]{0:T(128)S(1)}, s32[8]{0:T(128)}, u32[]{:S(2)}) copy-start(s32[8]{0:T(128)} %constant.120) | copy-start | bytes 100
  6.5 91.3 %copy-start.6 = (s32[128,8]{0,1:T(8,128)S(1)}, s32[128,8]{0,1:T(8,128)}, u32[]{:S(2)}) copy-start(s32[128,8]{0,1:T(8,128)} %param.17) | copy-start | bytes 12292
  6.5 91.4 %copy-start.7 = (f32[128,8]{0,1:T(8,128)S(1)}, f32[128,8]{0,1:T(8,128)}, u32[]{:S(2)}) copy-start(f32[128,8]{0,1:T(8,128)} %param.18) | copy-start | bytes 12292
  6.5 120.1 %copy-start.4 = (s32[32768]{0:T(1024)S(1)}, s32[32768]{0:T(1024)}, u32[]{:S(2)}) copy-start(s32[32768]{0:T(1024)} %param.16) | copy-start | bytes 393220
  6.5 91.3 %all-gather.10.cloned.1.call-start = ((), (), s32[]{:S(2)}) async-start(), calls=%async_computation.1 | async-start | bytes 10485760 | tf_op jit(solution)/shard_map/all_gather | solution.py:389
  7.3 135.5 %all-gather.8.cloned.1.call-start = ((), (), s32[]{:S(2)}) async-start(), calls=%async_computation | async-start | bytes 3932160 | tf_op jit(solution)/shard_map/all_gather | solution.py:387
  8.3 11.4 %collective-permute-start = (bf16[128,1024]{1,0:T(8,128)(2,1)S(1)}, bf16[128,1024]{1,0:T(8,128)(2,1)S(1)}, u32[]{:S(2)}, u32[]{:S(2)}) collective-permute-start(bf16[128,1024]{1,0:T(8,128)(2,1)S(1)} %bitcast.51), channel_id=1, source_target_pairs={{0,32},{8,40},{16,48},{24,56},{32,64},{40,72},{48,80},{56,88},{64,... | collective-permute-start | bytes 786440 | tf_op jit(solution)/shard_map/ppermute | solution.py:34
  19.7 10.5 %collective-permute-start.1 = (bf16[128,1024]{1,0:T(8,128)(2,1)S(1)}, bf16[128,1024]{1,0:T(8,128)(2,1)S(1)}, u32[]{:S(2)}, u32[]{:S(2)}) collective-permute-start(bf16[128,1024]{1,0:T(8,128)(2,1)S(1)} %collective-permute-done), channel_id=1, source_target_pairs={{0,32},{8,40},{16,48},{24,56},{32,64},{40,72},{48,80},{56,88},{64,... | collective-permute-start | bytes 786440 | tf_op jit(solution)/shard_map/ppermute | solution.py:34
  31.2 149.0 %all-gather.12.cloned.1.call-start = ((), (), s32[]{:S(2)}) async-start(), calls=%async_computation.2 | async-start | bytes 25165824 | tf_op jit(solution)/shard_map/all_gather | solution.py:390
  97.8 45.0 %copy-start.1 = (bf16[128,4096]{1,0:T(8,128)(2,1)S(1)}, bf16[128,4096]{1,0:T(8,128)(2,1)}, u32[]{:S(2)}) copy-start(bf16[128,4096]{1,0:T(8,128)(2,1)} %q_ref.1) | copy-start | bytes 3145732
  126.8 53.5 %copy-start.3 = (bf16[128,2048]{1,0:T(8,128)(2,1)S(1)}, bf16[128,2048]{1,0:T(8,128)(2,1)}, u32[]{:S(2)}) copy-start(bf16[128,2048]{1,0:T(8,128)(2,1)} %param.13) | copy-start | bytes 1572868
  142.8 1.9 copy-start
  180.2 8.3 %copy-start.5 = (f32[2048]{0:T(1024)S(1)}, f32[2048]{0:T(1024)}, u32[]{:S(2)}) copy-start(f32[2048]{0:T(1024)} %param.15) | copy-start | bytes 24580
  188.5 1.2 copy-start.2
Sparse Core Ops, SparseCore 0:
  9.2 88.5 all-gather.9
  99.6 43.1 all-gather.7
  144.6 35.5 all-gather.11

commit v2 on v1

--- a/solution.py
+++ b/solution.py
@@ -24,62 +24,325 @@
 MESH = pl.DeviceIdType.MESH
 
 
-def place_of(block):
-    sp, cp = block % (NZ * NY), block // (NZ * NY)
-    return sp * NX * NC + cp
-
-
-def from_behind(block, distance):
-    route = [(place_of(i), place_of((i + distance) % COUNT)) for i in range(COUNT)]
-    return lax.ppermute(block, MESH_AXES, route)
-
-
-def attention_kernel(q_ref, kv_ref, bias_ref, out_ref, k_ref, v_ref):
-    first = lax.axis_index("y")
+def front_kernel(
+    q_ref,
+    kv_ref,
+    bias_ref,
+    routes_ref,
+    residual_ref,
+    gain_ref,
+    weight_hbm,
+    summed_ref,
+    normed_ref,
+    routes_out,
+    window,
+    attended,
+    arrived,
+    weight,
+    share,
+    shares_in,
+    own,
+    routes_in,
+    own_sem,
+    w_send,
+    w_recv,
+    route_send,
+    route_recv,
+    z_send,
+    z_recv,
+    y_send,
+    y_recv,
+    att_send,
+    att_recv,
+    share_send,
+    share_recv,
+):
+    z, y, x, c = (lax.axis_index(name) for name in MESH_AXES)
+    model = residual_ref.shape[1]
     scale = math.log2(math.e) / math.sqrt(HD)
-    for g in range(KVH):
-        for b in range(SPAN // TOK):
-            block = first + b
-            rows = kv_ref[lax.rem(block, NY), block // NY]
-            k_ref[b * TOK : (b + 1) * TOK, :] = rows[:, g * 2 * HD : g * 2 * HD + HD]
-            v_ref[b * TOK : (b + 1) * TOK, :] = rows[:, g * 2 * HD + HD : (g + 1) * 2 * HD]
-
+
+    cp = x * NC + c
+    wrap = (z + 1) // NZ
+    cp_ahead = lax.rem(cp + wrap, NX * NC)
+    ahead = {"z": lax.rem(z + 1, NZ), "x": cp_ahead // NC, "c": lax.rem(cp_ahead, NC)}
+    wrap = 1 - (z + NZ - 1) // NZ
+    cp_behind = lax.rem(cp + NX * NC - wrap, NX * NC)
+    behind = {
+        "z": lax.rem(z + NZ - 1, NZ),
+        "x": cp_behind // NC,
+        "c": lax.rem(cp_behind, NC),
+    }
+
+    def along(axis, position, distance, size):
+        return {axis: lax.rem(position + distance, size)}
+
+    barrier = pltpu.get_barrier_semaphore()
+    others = [ahead, behind, {"c": 1 - c}]
+    others += [along("y", y, d, NY) for d in range(1, NY)]
+    others += [along("x", x, d, NX) for d in range(1, NX)]
+    others += [along("z", z, d, NZ) for d in range(1, NZ)]
+    for other in others:
+        pl.semaphore_signal(barrier, inc=1, device_id=other, device_id_type=MESH)
+    pl.semaphore_wait(barrier, len(others))
+
+    def remote(source, target, send, recv, device):
+        return pltpu.make_async_remote_copy(
+            src_ref=source,
+            dst_ref=target,
+            send_sem=send,
+            recv_sem=recv,
+            device_id=device,
+            device_id_type=MESH,
+        )
+
+    def hop(g, number):
+        source = window.at[g, (3 - number) * NY + y]
+        target = window.at[g, (2 - number) * NY + y]
+        return remote(
+            source, target, z_send.at[g, number - 1], z_recv.at[g, number - 1], ahead
+        )
+
+    def to_row(g, plane, d):
+        block = window.at[g, plane * NY + y]
+        return remote(
+            block,
+            block,
+            y_send.at[g, plane, d - 1],
+            y_recv.at[g, plane, d - 1],
+            along("y", y, d, NY),
+        )
+
+    def route_copy(d):
+        return remote(
+            routes_ref,
+            routes_in.at[BLOCK_ORDER.index(d)],
+            route_send.at[d],
+            route_recv.at[d],
+            along("z", z, d, NZ),
+        )
+
+    def rotated(n):
+        return lax.rem(x + 1 + n, KVH)
+
+    def first(n, carry):
+        g = rotated(n)
+        window[g, 2 * NY + y] = kv_ref[g]
+        hop(g, 1).start()
+        for d in range(1, NY):
+
+            @pl.when(y + d < NY)
+            def _():
+                to_row(g, 2, d).start()
+
+        return carry
+
+    lax.fori_loop(0, KVH, first, 0)
+
+    own_weight = pltpu.make_async_copy(weight_hbm, weight.at[c], own_sem)
+    own_weight.start()
+    given_weight = remote(weight_hbm, weight.at[c], w_send, w_recv, {"c": 1 - c})
+    given_weight.start()
+    for d in range(1, NZ):
+        route_copy(d).start()
+
+    def second(n, carry):
+        g = rotated(n)
+        hop(g, 1).wait_recv()
+        hop(g, 2).start()
+        for d in range(1, NY):
+            to_row(g, 1, d).start()
+        return carry
+
+    lax.fori_loop(0, KVH, second, 0)
+
+    def third(n, carry):
+        g = rotated(n)
+        hop(g, 2).wait_recv()
+        for d in range(1, NY):
+
+            @pl.when(y + d >= NY)
+            def _():
+                to_row(g, 0, d).start()
+
+        return carry
+
+    lax.fori_loop(0, KVH, third, 0)
+
+    own_weight.wait()
+    given_weight.wait()
+
+    def attend_copy(n):
+        g = rotated(n)
+        return remote(
+            attended.at[g], arrived.at[x], att_send.at[n], att_recv.at[n], {"x": g}
+        )
+
+    def source_of(n):
+        return lax.rem(x + NX - 1 - n, NX)
+
+    def share_copy(n):
+        source = source_of(n)
+        return remote(
+            share.at[n], shares_in.at[n], share_send.at[n], share_recv.at[n], {"x": source}
+        )
+
+    step = 512
+
+    def product(rows, columns):
+        total = jnp.dot(rows[:, : HG * HD], weight[0, :, columns], preferred_element_type=jnp.float32)
+        total += jnp.dot(rows[:, HG * HD :], weight[1, :, columns], preferred_element_type=jnp.float32)
+        return total
+
+    def project(n):
+        attend_copy(n).wait_recv()
+        rows = arrived[source_of(n)]
+
+        def part(m, carry):
+            columns = pl.ds(pl.multiple_of(m * step, step), step)
+            share[n, :, columns] = product(rows, columns).astype(jnp.bfloat16)
+            return carry
+
+        lax.fori_loop(0, model // step, part, 0)
+        share_copy(n).start()
+
+    def one_kv_head(n, carry):
+        g = rotated(n)
+        for d in range(1, NY):
+            to_row(g, 1, d).wait_recv()
+
+            @pl.when(y >= d)
+            def _():
+                to_row(g, 2, d).wait_recv()
+
+            @pl.when(y < d)
+            def _():
+                to_row(g, 0, d).wait_recv()
+
+        keys = window[g, pl.ds(y, SPAN // TOK), :, 0:HD].reshape(SPAN, HD)
+        values = window[g, pl.ds(y, SPAN // TOK), :, HD:].reshape(SPAN, HD)
         for i in range(GROUP):
-            head = g * GROUP + i
-            q = q_ref[:, head * HD : (head + 1) * HD]
+            q = q_ref[:, pl.ds(pl.multiple_of(g * GROUP * HD + i * HD, HD), HD)]
             scores = lax.dot_general(
-                q, k_ref[...], (((1,), (1,)), ((), ())), preferred_element_type=jnp.float32
+                q, keys, (((1,), (1,)), ((), ())), preferred_element_type=jnp.float32
             )
             scores = scores * scale + bias_ref[...]
             top = jnp.max(scores, axis=-1, keepdims=True)
             exponent = jnp.exp2(scores - top)
             denominator = jnp.sum(exponent, axis=-1, keepdims=True)
             numerator = jnp.dot(
-                exponent.astype(jnp.bfloat16), v_ref[...], preferred_element_type=jnp.float32
+                exponent.astype(jnp.bfloat16), values, preferred_element_type=jnp.float32
             )
-            group, inner = head // HG, head % HG
-            place = ((group % NC) * NX + group // NC) * HG + inner
-            out_ref[:, place * HD : (place + 1) * HD] = (numerator / denominator).astype(
-                jnp.bfloat16
-            )
-
-
-def attention(queries, kv_window, bias):
+            attended[g, :, i * HD : (i + 1) * HD] = (numerator / denominator).astype(jnp.bfloat16)
+
+        @pl.when(n < NX - 1)
+        def _():
+            attend_copy(n).start()
+
+        @pl.when(n > 0)
+        def _():
+            project(n - 1)
+
+        return carry
+
+    lax.fori_loop(0, KVH, one_kv_head, 0)
+
+    mine = attended[x]
+
+    def own_part(m, carry):
+        columns = pl.ds(pl.multiple_of(m * step, step), step)
+        own[:, columns] = product(mine, columns)
+        return carry
+
+    lax.fori_loop(0, model // step, own_part, 0)
+
+    for n in range(NX - 1):
+        share_copy(n).wait_recv()
+
+    def finish(m, carry):
+        rows = pl.ds(pl.multiple_of(m * 32, 32), 32)
+        summed = residual_ref[rows].astype(jnp.float32) + own[rows]
+        for n in range(NX - 1):
+            summed += shares_in[n, rows].astype(jnp.float32)
+        summed_ref[rows] = summed
+        mean = jnp.mean(summed * summed, axis=-1, keepdims=True)
+        normed_ref[rows] = (summed * lax.rsqrt(mean + 1e-06) * gain_ref[...]).astype(jnp.bfloat16)
+        return carry
+
+    lax.fori_loop(0, TOK // 32, finish, 0)
+
+    routes_in[0] = routes_ref[...]
+    for d in range(1, NZ):
+        route_copy(d).wait()
+    routes_out[...] = routes_in[...]
+
+    def drain(g, carry):
+        for number in (1, 2):
+            hop(g, number).wait_send()
+        for d in range(1, NY):
+            to_row(g, 1, d).wait_send()
+
+            @pl.when(y + d < NY)
+            def _():
+                to_row(g, 2, d).wait_send()
+
+            @pl.when(y + d >= NY)
+            def _():
+                to_row(g, 0, d).wait_send()
+
+        return carry
+
+    lax.fori_loop(0, KVH, drain, 0)
+    for n in range(NX - 1):
+        attend_copy(n).wait_send()
+        share_copy(n).wait_send()
+
+
+def front(queries, keyvals, bias, routes, residual, gain, out_weight):
+    model = residual.shape[1]
+    vmem, hbm = pl.BlockSpec(memory_space=pltpu.VMEM), pl.BlockSpec(memory_space=pl.ANY)
+    dma = pltpu.SemaphoreType.DMA
+    half = HEADS * HD // NX
+    bf16, f32 = jnp.bfloat16, jnp.float32
     return pl.pallas_call(
-        attention_kernel,
-        out_shape=jax.ShapeDtypeStruct(queries.shape, jnp.bfloat16),
-        in_specs=[pl.BlockSpec(memory_space=pltpu.VMEM)] * 3,
-        out_specs=pl.BlockSpec(memory_space=pltpu.VMEM),
+        front_kernel,
+        out_shape=(
+            jax.ShapeDtypeStruct((TOK, model), f32),
+            jax.ShapeDtypeStruct((TOK, model), bf16),
+            jax.ShapeDtypeStruct((NZ,) + routes.shape, f32),
+        ),
+        in_specs=[vmem] * 6 + [hbm],
+        out_specs=(vmem,) * 3,
         scratch_shapes=[
-            pltpu.VMEM((SPAN, HD), jnp.bfloat16),
-            pltpu.VMEM((SPAN, HD), jnp.bfloat16),
+            pltpu.VMEM((KVH, 3 * NY, TOK, 2 * HD), bf16),
+            pltpu.VMEM((KVH, TOK, half), bf16),
+            pltpu.VMEM((NX, TOK, half), bf16),
+            pltpu.VMEM((NC,) + out_weight.shape, bf16),
+            pltpu.VMEM((NX - 1, TOK, model), bf16),
+            pltpu.VMEM((NX - 1, TOK, model), bf16),
+            pltpu.VMEM((TOK, model), f32),
+            pltpu.VMEM((NZ,) + routes.shape, f32),
+            dma,
+            dma,
+            dma,
+            dma((NZ,)),
+            dma((NZ,)),
+            dma((KVH, 2)),
+            dma((KVH, 2)),
+            dma((KVH, 3, NY - 1)),
+            dma((KVH, 3, NY - 1)),
+            dma((NX - 1,)),
+            dma((NX - 1,)),
+            dma((NX - 1,)),
+            dma((NX - 1,)),
         ],
-        compiler_params=pltpu.CompilerParams(vmem_limit_bytes=40 * 2**20),
+        compiler_params=pltpu.CompilerParams(
+            collective_id=2, has_side_effects=True, vmem_limit_bytes=48 * 2**20
+        ),
         cost_estimate=pl.CostEstimate(
-            flops=4 * HEADS * TOK * SPAN * HD, bytes_accessed=8 * 2**20, transcendentals=HEADS * TOK * SPAN
+            flops=4 * 10**9, bytes_accessed=8 * 2**20, transcendentals=HEADS * TOK * SPAN
         ),
-        name="attention",
-    )(queries, kv_window, bias)
+        name="front",
+    )(queries, keyvals, bias, routes, residual, gain, out_weight)
 
 
 def moe_kernel(
@@ -381,30 +644,31 @@
     z, y = lax.axis_index("z"), lax.axis_index("y")
     number = ((lax.axis_index("x") * NC + lax.axis_index("c")) * NZ + z) * NY + y
 
-    kv = keyvals.reshape(TOK, -1)
-    back1 = from_behind(kv, NY)
-    back2 = from_behind(back1, NY)
-    kv_window = lax.all_gather(jnp.stack([back2, back1, kv]), "y")
-
-    weight = lax.all_gather(out_weight, "x")
-    weight = lax.all_gather(weight, "c").reshape(-1, model)
-
+    padded = jnp.concatenate([jnp.full((DOC_MAX,), -1, jnp.int32), doc_ids], axis=0)
+    key_docs = lax.dynamic_slice_in_dim(padded, number * TOK, SPAN, 0)
+    query_docs = key_docs[DOC_MAX:]
+    allowed = (key_docs[None, :] == query_docs[:, None]) & (
+        jnp.arange(SPAN)[None, :] <= jnp.arange(TOK)[:, None] + DOC_MAX
+    )
+    bias = jnp.where(allowed, 0.0, -1e30).astype(jnp.float32)
     routes = jnp.concatenate([expert_ids.astype(jnp.float32), route_weights], axis=1)
-    routes = lax.all_gather(routes, "z")
-    routes = jnp.take(routes, lax.rem(z + NZ - jnp.array(BLOCK_ORDER), NZ), axis=0)
-    ids = routes[:, :, :8].astype(jnp.int32)
+    summed, normed, routes = front(
+        queries, keyvals.transpose(1, 0, 2), bias, routes.T, residual, norm_gain[None], out_weight
+    )
+
+    ids = routes[:, :8].astype(jnp.int32)
     plane_experts = z * PLANE + jnp.arange(PLANE, dtype=jnp.int32)
-    hit = ids[:, :, :, None] == plane_experts
+    hit = ids[:, None] == plane_experts[:, None, None]
     chosen = jnp.any(hit, axis=2)
-    weight_of = jnp.sum(jnp.where(hit, routes[:, :, 8:, None], 0.0), axis=2)
-    earlier = jnp.tril(jnp.ones((TOK, TOK), jnp.bfloat16), -1)
+    weight_of = jnp.sum(jnp.where(hit, routes[:, None, 8:], 0.0), axis=2)
+    earlier = jnp.triu(jnp.ones((TOK, TOK), jnp.bfloat16), 1)
     rank = jnp.einsum(
-        "ts,bse->bte", earlier, chosen.astype(jnp.bfloat16), preferred_element_type=jnp.float32
+        "bes,st->bet", chosen.astype(jnp.bfloat16), earlier, preferred_element_type=jnp.float32
     ).astype(jnp.int32)
     slot = jnp.where(chosen, rank, CAP)
 
     def by_expert(values):
-        values = values.reshape(4, 2, TOK, PLANE).transpose(0, 3, 1, 2)
+        values = values.reshape(4, 2, PLANE, TOK).transpose(0, 2, 1, 3)
         return values.reshape(4, PLANE, 1, 1, 2 * TOK)
 
     row = jnp.arange(2 * CAP, dtype=jnp.int32)[:, None]
@@ -414,22 +678,6 @@
     spread = jnp.where(taken, by_expert(weight_of)[:, :, 0], 0.0).reshape(4, 2 * TOK, 2 * TOK)
     spread_high = lax.reduce_precision(spread, 8, 7)
     spread = jnp.stack([spread_high, spread - spread_high]).astype(jnp.bfloat16)
-
-    padded = jnp.concatenate([jnp.full((DOC_MAX,), -1, jnp.int32), doc_ids], axis=0)
-    key_docs = lax.dynamic_slice_in_dim(padded, number * TOK, SPAN, 0)
-    query_docs = key_docs[DOC_MAX:]
-    allowed = (key_docs[None, :] == query_docs[:, None]) & (
-        jnp.arange(SPAN)[None, :] <= jnp.arange(TOK)[:, None] + DOC_MAX
-    )
-    bias = jnp.where(allowed, 0.0, -1e30).astype(jnp.float32)
-    attended = attention(queries, kv_window, bias)
-
-    summed = residual.astype(jnp.float32) + jnp.dot(
-        attended, weight, preferred_element_type=jnp.float32
-    )
-    normed = (
-        summed * lax.rsqrt(jnp.mean(summed * summed, axis=-1, keepdims=True) + 1e-06) * norm_gain
-    ).astype(jnp.bfloat16)
 
     return moe(normed, summed, pick, spread, expert_in, expert_out)
 

time: 351 us -> 258 us (0.74)
  waiting for transfers between devices: 122 us -> 0 us
  Pallas kernels: 164 us -> 240 us
  blocking collectives: 26.1 us -> 0 us
  between operations: 13.4 us -> 0.15 us
  matrix products: 8.48 us -> 0.14 us
    all_gather x3 -> x0, waiting for transfers between devices: 103 us -> none  [the longest x1 66.5 us: on_device(): weight = lax.all_gather(out_weight, 'x')]
    pallas_call x1, Pallas kernels: 13.3 us -> 77.7 us  [front(): pl.pallas_call(front_kernel, out_shape=(jax.ShapeDtypeStruct((TOK, model)...]
    all_gather x1 -> x0, blocking collectives: 26.1 us -> none  [on_device(): routes = lax.all_gather(routes, 'z')]
    ppermute x2 -> x0, waiting for transfers between devices: 18.8 us -> none  [from_behind(): return lax.ppermute(block, MESH_AXES, route)]
    pallas_call x1, Pallas kernels: 151 us -> 162 us  [moe(): pl.pallas_call(moe_kernel, out_shape=jax.ShapeDtypeStruct(normed.shape, j...]
    dot_general x2 -> x1, matrix products: 8.48 us -> 0.14 us  [on_device(): jnp.einsum('bes,st->bet', chosen.astype(jnp.bfloat16), earlier, preferred...]
    unnamed x20 -> x14, local copies, waits for them, and re-layouts: 4.85 us -> 9.16 us
  transfers between devices with their start and end apart: 5 -> 0, of which waited for: 5 -> 0; matrix products, arithmetic and copies ran while one was open for 2% -> 0% of each run, Pallas kernels for 4% -> 0%
where the time goes in v2:
time: 258 us; the launch traced here: 256 us
  Pallas kernels  240 us (93%)
  local copies, waits for them, and re-layouts  10.3 us (4%)
  other arithmetic  5.35 us (2%)
    pallas_call x1, Pallas kernels, moe(): pl.pallas_call(moe_kernel, out_shape=jax.ShapeDtypeStruct(normed.shape, j...  162 us
    pallas_call x1, Pallas kernels, front(): pl.pallas_call(front_kernel, out_shape=(jax.ShapeDtypeStruct((TOK, model)...  77.7 us
    unnamed x14, local copies, waits for them, and re-layouts  9.16 us

profile of v2, /device:TPU:2, one launch (start us, length us, event | category | flops | bytes accessed | tf_op | source)
XLA Modules:
  0.0 255.8 jit_solution(14414038171191761679)
XLA Ops:
  0.0 0.8 pad_dynamic-slice_fusion
  0.8 0.8 pad_dynamic-slice_fusion.1
  1.5 0.2 fusion.5.bias_ref
  1.7 1.0 copy.24
  2.7 0.7 convert_element_type.15
  3.4 0.7 maximum_bitcast_fusion.routes_ref
  4.1 1.6 copy-done
  5.7 1.2 copy-done.1
  6.9 1.0 copy-done.2
  8.0 0.7 copy-done.3
  8.7 77.7 %front.1 = (f32[128,2048]{1,0:T(8,128)S(1)}, bf16[128,2048]{1,0:T(8,128)(2,1)S(1)}, f32[8,16,128]{2,1,0:T(8,128)S(1)}) custom-call(bf16[128,4096]{1,0:T(8,128)(2,1)S(1)} %copy-done.1, bf16[4,128,256]{2,1,0:T(8,128)(2,1)S(1)} %bitcast.30, f32[128,1152]{1,0:T(8,128)S(1)} %fusion.5.bias_ref, f32[16,128]{1,0:T(8,128)S(1)} %maximum_bitcast_fusion.routes_ref, ...), custom_call_target="tpu_custom_call" | custom-call | flops 4000000000 | bytes 8388608 | tf_op jit(solution)/shard_map/front/pallas_call | solution.py:306
  86.4 1.0 copy-done.4
  87.4 0.8 copy-done.5
  88.2 0.2 fusion.6
  88.4 0.1 broadcast_in_dim.70
  88.5 0.2 compare_reduce_fusion
  88.8 0.1 fusion
  89.0 0.1 eq.102
  89.2 0.1 eq.105
  89.3 0.3 reduce-precision_convert_fusion
  89.7 1.1 pad_maximum_fusion.spread_ref
  90.8 1.0 fusion.3.pick_ref
  91.8 162.1 %moe.1 = bf16[128,2048]{1,0:T(8,128)(2,1)} custom-call(bf16[128,2048]{1,0:T(8,128)(2,1)} %copy-done.5, f32[128,2048]{1,0:T(8,128)} %copy-done.4, bf16[4,256,256]{2,1,0:T(8,128)(2,1)} %fusion.3.pick_ref, bf16[2,4,256,256]{3,2,1,0:T(8,128)(2,1)} %pad_maximum_fusion.spread_ref, bf16[1,2048,768]{2,1,0:T(8,128)(2,1)} %w_in_hbm.1, bf16[1,384,2048]{2,1,0:T(8,128)(2,1)} %w_out_hbm.1), custom_call_target="tpu_custom_call" | custom-call | flops 10000000000 | bytes 12582912 | tf_op jit(solution)/shard_map/moe/pallas_call | solution.py:593
  253.9 1.9 copy.28
  (17 shorter events, 0.2 us)
Async XLA Ops:
  4.1 1.6 copy-start
  5.7 1.2 copy-start.1
  6.9 1.0 copy-start.2
  8.0 0.7 copy-start.3
  86.4 1.0 copy-start.4
  87.4 0.8 copy-start.5

commit v3 on v2

v3 whole, which is shorter than its diff:
```python
import math

import jax
import jax.numpy as jnp
from jax import lax
from jax.experimental import pallas as pl
from jax.experimental.pallas import tpu as pltpu
from jax.sharding import Mesh, PartitionSpec as P

NZ, NY, NX, NC = 8, 4, 4, 2
TOK = 128
HD = 128
KVH = 4
HEADS = 32
GROUP = HEADS // KVH
HG = 4
CAP = 8
DOC_MAX = 1024
SPAN = DOC_MAX + TOK
MESH_AXES = ("z", "y", "x", "c")
COUNT = NZ * NY * NX * NC
PLANE = NY * NX
MESH = pl.DeviceIdType.MESH


def layer_kernel(
    queries_hbm,
    kv_ref,
    key_docs_ref,
    query_docs_ref,
    routes_ref,
    residual_hbm,
    gain_ref,
    weight_hbm,
    w_in_hbm,
    w_out_hbm,
    out_ref,
    queries,
    residual,
    bias,
    window,
    attended,
    arrived,
    weight,
    share,
    shares_in,
    own,
    routes_in,
    col,
    stage,
    recv,
    back,
    acc,
    ring,
    home,
    slot_of,
    weight_of,
    w_in,
    w_out,
    load_sem,
    given_send,
    given_recv,
    route_send,
    route_recv,
    z_send,
    z_recv,
    y_send,
    y_recv,
    att_send,
    att_recv,
    share_send,
    share_recv,
    own_sem,
    w_send,
    w_recv,
    col_send,
    col_recv,
    out_send,
    out_recv,
    back_send,
    back_recv,
    ring_send,
    ring_recv,
):
    z, y, x, c = (lax.axis_index(name) for name in MESH_AXES)
    model = residual.shape[1]
    wide = model // 2
    scale = math.log2(math.e) / math.sqrt(HD)

    cp = x * NC + c
    wrap = (z + 1) // NZ
    cp_ahead = lax.rem(cp + wrap, NX * NC)
    ahead = {"z": lax.rem(z + 1, NZ), "x": cp_ahead // NC, "c": lax.rem(cp_ahead, NC)}
    wrap = 1 - (z + NZ - 1) // NZ
    cp_behind = lax.rem(cp + NX * NC - wrap, NX * NC)
    behind = {
        "z": lax.rem(z + NZ - 1, NZ),
        "x": cp_behind // NC,
        "c": lax.rem(cp_behind, NC),
    }

    def along(axis, position, distance, size):
        return {axis: lax.rem(position + distance, size)}

    def peer(k):
        other_y, other_x = lax.rem(y + k // NX, NY), lax.rem(x + k % NX, NX)
        return {"y": other_y, "x": other_x}, other_y * NX + other_x

    barrier = pltpu.get_barrier_semaphore()

    def greet(k, carry):
        pl.semaphore_signal(barrier, inc=1, device_id=peer(k)[0], device_id_type=MESH)
        return carry

    lax.fori_loop(1, PLANE, greet, 0)
    others = [ahead, behind, {"c": 1 - c}]
    others += [along("z", z, d, NZ) for d in range(1, NZ)]
    for other in others:
        pl.semaphore_signal(barrier, inc=1, device_id=other, device_id_type=MESH)
    pl.semaphore_wait(barrier, PLANE - 1 + len(others))

    def remote(source, target, send, recv, device):
        return pltpu.make_async_remote_copy(
            src_ref=source,
            dst_ref=target,
            send_sem=send,
            recv_sem=recv,
            device_id=device,
            device_id_type=MESH,
        )

    def hop(g, number):
        source = window.at[g, (3 - number) * NY + y]
        target = window.at[g, (2 - number) * NY + y]
        return remote(
            source, target, z_send.at[g, number - 1], z_recv.at[g, number - 1], ahead
        )

    def to_row(g, plane, d):
        block = window.at[g, plane * NY + y]
        return remote(
            block,
            block,
            y_send.at[g, plane, d - 1],
            y_recv.at[g, plane, d - 1],
            along("y", y, d, NY),
        )

    def route_copy(d):
        return remote(
            routes_ref,
            routes_in.at[d],
            route_send.at[d],
            route_recv.at[d],
            along("z", z, d, NZ),
        )

    def rotated(n):
        return lax.rem(x + 1 + n, KVH)

    def first(n, carry):
        g = rotated(n)
        window[g, 2 * NY + y] = kv_ref[g]
        hop(g, 1).start()
        for d in range(1, NY):

            @pl.when(y + d < NY)
            def _():
                to_row(g, 2, d).start()

        return carry

    lax.fori_loop(0, KVH, first, 0)

    for d in range(1, NZ):
        route_copy(d).start()
    loads = [
        pltpu.make_async_copy(queries_hbm, queries, load_sem.at[0]),
        pltpu.make_async_copy(residual_hbm, residual, load_sem.at[1]),
        pltpu.make_async_copy(weight_hbm, weight.at[c], load_sem.at[2]),
        remote(weight_hbm, weight.at[c], given_send, given_recv, {"c": 1 - c}),
    ]
    for load in loads:
        load.start()

    def second(n, carry):
        g = rotated(n)
        hop(g, 1).wait_recv()
        hop(g, 2).start()
        for d in range(1, NY):
            to_row(g, 1, d).start()
        return carry

    lax.fori_loop(0, KVH, second, 0)

    keys_at = lax.broadcasted_iota(jnp.int32, (TOK, SPAN), 1)
    tokens_at = lax.broadcasted_iota(jnp.int32, (TOK, SPAN), 0) + DOC_MAX
    allowed = (key_docs_ref[...] == query_docs_ref[...]) & (keys_at <= tokens_at)
    bias[...] = jnp.where(allowed, 0.0, -1e30)

    def third(n, carry):
        g = rotated(n)
        hop(g, 2).wait_recv()
        for d in range(1, NY):

            @pl.when(y + d >= NY)
            def _():
                to_row(g, 0, d).start()

        return carry

    lax.fori_loop(0, KVH, third, 0)

    weight_copies = []
    for n, (hbm, vmem) in enumerate(((w_in_hbm, w_in), (w_out_hbm, w_out))):
        own_part = pltpu.make_async_copy(hbm.at[0], vmem.at[c], own_sem.at[n])
        given = remote(hbm.at[0], vmem.at[c], w_send.at[n], w_recv.at[n], {"c": 1 - c})
        own_part.start()
        given.start()
        weight_copies += [own_part, given]

    for load in loads:
        load.wait()

    def attend_copy(n):
        g = rotated(n)
        return remote(
            attended.at[g], arrived.at[x], att_send.at[n], att_recv.at[n], {"x": g}
        )

    def source_of(n):
        return lax.rem(x + NX - 1 - n, NX)

    def share_copy(n):
        source = source_of(n)
        return remote(
            share.at[n], shares_in.at[n], share_send.at[n], share_recv.at[n], {"x": source}
        )

    step = 512

    def product(rows, columns):
        total = jnp.dot(rows[:, : HG * HD], weight[0, :, columns], preferred_element_type=jnp.float32)
        total += jnp.dot(rows[:, HG * HD :], weight[1, :, columns], preferred_element_type=jnp.float32)
        return total

    def project(n):
        attend_copy(n).wait_recv()
        rows = arrived[source_of(n)]

        def part(m, carry):
            columns = pl.ds(pl.multiple_of(m * step, step), step)
            share[n, :, columns] = product(rows, columns).astype(jnp.bfloat16)
            return carry

        lax.fori_loop(0, model // step, part, 0)
        share_copy(n).start()

    def one_kv_head(n, carry):
        g = rotated(n)
        for d in range(1, NY):
            to_row(g, 1, d).wait_recv()

            @pl.when(y >= d)
            def _():
                to_row(g, 2, d).wait_recv()

            @pl.when(y < d)
            def _():
                to_row(g, 0, d).wait_recv()

        keys = window[g, pl.ds(y, SPAN // TOK), :, 0:HD].reshape(SPAN, HD)
        values = window[g, pl.ds(y, SPAN // TOK), :, HD:].reshape(SPAN, HD)
        for i in range(0, GROUP, 2):
            first_column = g * GROUP * HD + i * HD
            q = [
                queries[:, pl.ds(pl.multiple_of(first_column + k * HD, HD), HD)] for k in range(2)
            ]
            scores = lax.dot_general(
                jnp.concatenate(q, axis=0),
                keys,
                (((1,), (1,)), ((), ())),
                preferred_element_type=jnp.float32,
            )
            scores = scores.reshape(2, TOK, SPAN) * scale + bias[...]
            top = jnp.max(scores, axis=-1, keepdims=True)
            exponent = jnp.exp2(scores - top)
            denominator = jnp.sum(exponent, axis=-1, keepdims=True)
            numerator = jnp.dot(
                exponent.astype(jnp.bfloat16).reshape(2 * TOK, SPAN),
                values,
                preferred_element_type=jnp.float32,
            )
            result = (numerator.reshape(2, TOK, HD) / denominator).astype(jnp.bfloat16)
            for k in range(2):
                attended[g, :, (i + k) * HD : (i + k + 1) * HD] = result[k]

        @pl.when(n < NX - 1)
        def _():
            attend_copy(n).start()

        @pl.when(n > 0)
        def _():
            project(n - 1)

        return carry

    lax.fori_loop(0, KVH, one_kv_head, 0)

    mine = attended[x]

    def own_product(m, carry):
        columns = pl.ds(pl.multiple_of(m * step, step), step)
        own[:, columns] = product(mine, columns)
        return carry

    lax.fori_loop(0, model // step, own_product, 0)

    for n in range(NX - 1):
        share_copy(n).wait_recv()

    def normalize(m, carry):
        rows = pl.ds(pl.multiple_of(m * 32, 32), 32)
        summed = residual[rows].astype(jnp.float32) + own[rows]
        for n in range(NX - 1):
            summed += shares_in[n, rows].astype(jnp.float32)
        own[rows] = summed
        mean = jnp.mean(summed * summed, axis=-1, keepdims=True)
        normed = (summed * lax.rsqrt(mean + 1e-06) * gain_ref[...]).astype(jnp.bfloat16)
        col[0, rows] = normed[:, :wide]
        col[0, pl.ds(pl.multiple_of(TOK + m * 32, 32), 32)] = normed[:, wide:]
        return carry

    lax.fori_loop(0, TOK // 32, normalize, 0)

    place = y * NX + x
    right, left = lax.rem(z + 1, NZ), lax.rem(z + NZ - 1, NZ)

    def ring_copy(direction, n, side):
        source, target = (n - 1, n) if direction == 0 else ((NZ + 1 - n) % NZ, NZ - n)
        rows = pl.ds(side * TOK, TOK)
        return remote(
            col.at[source, rows],
            col.at[target, rows],
            col_send.at[direction, n - 1, side],
            col_recv.at[direction, n - 1, side],
            {"z": right if direction == 0 else left},
        )

    steps = [
        (n, side, direction)
        for n in range(1, 5)
        for side in range(2)
        for direction in range(2)
        if n < 4 or side == direction
    ]
    for n, side, direction in steps:
        if n == 1:
            ring_copy(direction, 1, side).start()

    def far_first(k):
        return (2 + k) * (1 - k // 2) + (3 - k) * (k // 2)

    def exchange(source, target, sends, recvs, r):
        def send(k, carry):
            device, expert = peer(far_first(k // NX) * NX + far_first(k % NX))
            remote(
                source.at[r, expert], target.at[r, place], sends.at[r], recvs.at[r], device
            ).start()
            return carry

        lax.fori_loop(0, PLANE - 1, send, 0)
        target[r, place] = source[r, place]

    def whole(source, target, sends, recvs, r):
        others = pl.ds(0, PLANE - 1)
        return remote(
            source.at[r, others], target.at[r, others], sends.at[r], recvs.at[r], {"c": c}
        )

    token = lax.broadcasted_iota(jnp.int32, (TOK, TOK), 0)
    earlier = (token < lax.broadcasted_iota(jnp.int32, (TOK, TOK), 1)).astype(jnp.bfloat16)
    expert_row = lax.broadcasted_iota(jnp.int32, (PLANE, TOK), 0) + z * PLANE
    expert_row = expert_row.astype(jnp.float32)
    slot_row = lax.rem(lax.broadcasted_iota(jnp.int32, (PLANE * 2 * CAP, TOK), 0), 2 * CAP)
    side_row = slot_row // CAP
    slot_row = lax.rem(slot_row, CAP).astype(jnp.float32)

    def slots(r):
        chosen = jnp.zeros((PLANE, TOK), jnp.float32)
        weight = jnp.zeros((PLANE, TOK), jnp.float32)
        for j in range(8):
            hit = routes_in[r, j : j + 1, :] == expert_row
            chosen = jnp.where(hit, 1.0, chosen)
            weight = jnp.where(hit, routes_in[r, 8 + j : 9 + j, :], weight)
        rank = jnp.dot(
            chosen.astype(jnp.bfloat16), earlier, preferred_element_type=jnp.float32
        )
        slot_of[r] = jnp.where(chosen > 0.0, jnp.minimum(rank, float(CAP)), float(CAP))
        weight_of[r] = weight

    def by_slot(values):
        rows = jnp.broadcast_to(values[:, None, :], (PLANE, 2 * CAP, TOK))
        return rows.reshape(PLANE * 2 * CAP, TOK)

    def taken(r):
        return by_slot(slot_of[r]) == slot_row

    def both_sides(values):
        low, high = jnp.where(side_row == 0, values, 0.0), jnp.where(side_row == 1, values, 0.0)
        return jnp.concatenate([low, high], axis=1)

    def dispatch(r):
        slots(r)
        pick = both_sides(jnp.where(taken(r), 1.0, 0.0)).astype(jnp.bfloat16)

        def select(n, carry):
            columns = pl.ds(pl.multiple_of(n * step, step), step)
            rows = jnp.dot(pick, col[r, :, columns], preferred_element_type=jnp.float32)
            stage[r, :, :, columns] = rows.reshape(PLANE, 2 * CAP, step).astype(jnp.bfloat16)
            return carry

        lax.fori_loop(0, wide // step, select, 0)
        exchange(stage, recv, out_send, out_recv, r)

    def expert(blocks):
        rows = []
        for r in blocks:
            whole(stage, recv, out_send, out_recv, r).wait_recv()
            came = recv[r].astype(jnp.float32).reshape(PLANE, 2, CAP, wide)
            sides = [came[:, side].reshape(PLANE * CAP, wide) for side in range(2)]
            rows.append(jnp.concatenate(sides, axis=1).astype(jnp.bfloat16))
        rows = jnp.concatenate(rows, axis=0) if len(rows) > 1 else rows[0]
        width = w_out.shape[1]
        acts = []
        for p in range(2):
            gate_up = jnp.dot(rows, w_in[p], preferred_element_type=jnp.float32)
            gate, up = gate_up[:, :width], gate_up[:, width:]
            acts.append((gate / (1.0 + jnp.exp(-gate)) * up).astype(jnp.bfloat16))

        def down(n, carry):
            sides = []
            for side in range(2):
                columns = pl.ds(pl.multiple_of(side * wide + n * step, step), step)
                total = jnp.dot(acts[0], w_out[0, :, columns], preferred_element_type=jnp.float32)
                total += jnp.dot(acts[1], w_out[1, :, columns], preferred_element_type=jnp.float32)
                sides.append(total.reshape(len(blocks), PLANE, 1, CAP, step))
            total = jnp.concatenate(sides, axis=2).reshape(len(blocks), PLANE, 2 * CAP, step)
            columns = pl.ds(pl.multiple_of(n * step, step), step)
            for i, r in enumerate(blocks):
                recv[r, :, :, columns] = total[i].astype(jnp.bfloat16)
            return carry

        lax.fori_loop(0, wide // step, down, 0)

    routes_in[0] = routes_ref[...]
    for d in range(1, NZ):
        route_copy(d).wait()

    dispatch(0)

    groups = [(0,), (1, 7), (2, 6), (3, 5), (4,)]
    for n in range(1, 5):
        for at, side, direction in steps:
            if at == n:
                ring_copy(direction, n, side).wait_recv()
                if (n + 1, side, direction) in steps:
                    ring_copy(direction, n + 1, side).start()
        for r in groups[n]:
            dispatch(r)
        if n == 1:
            for copy in weight_copies:
                copy.wait()
        expert(groups[n - 1])
    expert(groups[4])

    def give_back(n):
        for r in groups[n]:
            exchange(recv, back, back_send, back_recv, r)

    def sum_copy(direction, n, side):
        source, target = (n, n - 1) if direction == 0 else (NZ - n, NZ + 1 - n)
        rows = pl.ds(side * TOK, TOK)
        return remote(
            acc.at[source, rows],
            ring.at[target, rows],
            ring_send.at[direction, n - 1, side],
            ring_recv.at[direction, n - 1, side],
            {"z": left if direction == 0 else right},
        )

    def weigh(r, sums):
        spread = both_sides(jnp.where(taken(r), by_slot(weight_of[r]), 0.0))
        high = spread.astype(jnp.bfloat16)
        low = (spread - high.astype(jnp.float32)).astype(jnp.bfloat16)

        def part(n, carry):
            columns = pl.ds(pl.multiple_of(n * step, step), step)
            rows = back[r, :, :, columns].reshape(PLANE * 2 * CAP, step)
            total = jnp.zeros((2 * TOK, step), jnp.float32)
            for matrix in (high, low):
                total += lax.dot_general(
                    matrix, rows, (((0,), (0,)), ((), ())), preferred_element_type=jnp.float32
                )
            sums[:, columns] = total
            return carry

        lax.fori_loop(0, wide // step, part, 0)

    give_back(4)
    give_back(3)
    for n in (4, 3, 2, 1, 0):
        for k, r in enumerate(groups[n]):
            whole(recv, back, back_send, back_recv, r).wait_recv()
            weigh(r, home.at[k])
        if n == 0:
            break
        for at, side, direction in steps:
            if at != n:
                continue
            r = n if direction == 0 else NZ - n
            rows = pl.ds(side * TOK, TOK)
            total = home[0 if n == 4 else direction, rows]
            if (n + 1, side, direction) in steps:
                sum_copy(direction, n + 1, side).wait_recv()
                total += ring[r, rows].astype(jnp.float32)
            acc[r, rows] = total.astype(jnp.bfloat16)
            sum_copy(direction, n, side).start()
        if n >= 2:
            give_back(n - 2)

    for side in range(2):
        rows = pl.ds(side * TOK, TOK)
        columns = pl.ds(side * wide, wide)
        moe_sum = home[0, rows]
        for direction in range(2):
            sum_copy(direction, 1, side).wait_recv()
            moe_sum += ring[direction * NZ, rows].astype(jnp.float32)
        out_ref[:, columns] = (own[:, columns] + moe_sum).astype(jnp.bfloat16)

    for r in range(NZ):
        whole(stage, recv, out_send, out_recv, r).wait_send()
        whole(recv, back, back_send, back_recv, r).wait_send()
    for n, side, direction in steps:
        ring_copy(direction, n, side).wait_send()
        sum_copy(direction, n, side).wait_send()

    def drain(g, carry):
        for number in (1, 2):
            hop(g, number).wait_send()
        for d in range(1, NY):
            to_row(g, 1, d).wait_send()

            @pl.when(y + d < NY)
            def _():
                to_row(g, 2, d).wait_send()

            @pl.when(y + d >= NY)
            def _():
                to_row(g, 0, d).wait_send()

        return carry

    lax.fori_loop(0, KVH, drain, 0)
    for n in range(NX - 1):
        attend_copy(n).wait_send()
        share_copy(n).wait_send()


def layer(
    queries, kv, key_docs, query_docs, routes, residual, gain, out_weight, expert_in, expert_out
):
    model = residual.shape[1]
    vmem, hbm = pl.BlockSpec(memory_space=pltpu.VMEM), pl.BlockSpec(memory_space=pl.ANY)
    dma = pltpu.SemaphoreType.DMA
    half = HEADS * HD // NX
    bf16, f32 = jnp.bfloat16, jnp.float32
    slots = (NZ, PLANE, 2 * CAP, model // 2)
    blocks = (NZ, 2 * TOK, model // 2)
    return pl.pallas_call(
        layer_kernel,
        out_shape=jax.ShapeDtypeStruct(residual.shape, bf16),
        in_specs=[hbm, vmem, vmem, vmem, vmem, hbm, vmem, hbm, hbm, hbm],
        out_specs=vmem,
        scratch_shapes=[
            pltpu.VMEM(queries.shape, bf16),
            pltpu.VMEM(residual.shape, bf16),
            pltpu.VMEM((TOK, SPAN), f32),
            pltpu.VMEM((KVH, 3 * NY, TOK, 2 * HD), bf16),
            pltpu.VMEM((KVH, TOK, half), bf16),
            pltpu.VMEM((NX, TOK, half), bf16),
            pltpu.VMEM((NC,) + out_weight.shape, bf16),
            pltpu.VMEM((NX - 1, TOK, model), bf16),
            pltpu.VMEM((NX - 1, TOK, model), bf16),
            pltpu.VMEM((TOK, model), f32),
            pltpu.VMEM((NZ,) + routes.shape, f32),
            pltpu.VMEM(blocks, bf16),
            pltpu.VMEM(slots, bf16),
            pltpu.VMEM(slots, bf16),
            pltpu.VMEM(slots, bf16),
            pltpu.VMEM(blocks, bf16),
            pltpu.VMEM((NZ + 1,) + blocks[1:], bf16),
            pltpu.VMEM((2,) + blocks[1:], f32),
            pltpu.VMEM((NZ, PLANE, TOK), f32),
            pltpu.VMEM((NZ, PLANE, TOK), f32),
            pltpu.VMEM((2,) + expert_in.shape[1:], bf16),
            pltpu.VMEM((2,) + expert_out.shape[1:], bf16),
            dma((3,)),
            dma,
            dma,
            dma((NZ,)),
            dma((NZ,)),
            dma((KVH, 2)),
            dma((KVH, 2)),
            dma((KVH, 3, NY - 1)),
            dma((KVH, 3, NY - 1)),
            dma((NX - 1,)),
            dma((NX - 1,)),
            dma((NX - 1,)),
            dma((NX - 1,)),
            dma((2,)),
            dma((2,)),
            dma((2,)),
            dma((2, 4, 2)),
            dma((2, 4, 2)),
            dma((NZ,)),
            dma((NZ,)),
            dma((NZ,)),
            dma((NZ,)),
            dma((2, 4, 2)),
            dma((2, 4, 2)),
        ],
        compiler_params=pltpu.CompilerParams(
            collective_id=1, has_side_effects=True, vmem_limit_bytes=60 * 2**20
        ),
        cost_estimate=pl.CostEstimate(
            flops=14 * 10**9, bytes_accessed=20 * 2**20, transcendentals=HEADS * TOK * SPAN
        ),
        name="layer",
    )(queries, kv, key_docs, query_docs, routes, residual, gain, out_weight, expert_in, expert_out)


def on_device(
    queries,
    keyvals,
    residual,
    out_weight,
    norm_gain,
    doc_ids,
    expert_ids,
    route_weights,
    expert_in,
    expert_out,
):
    number = ((lax.axis_index("x") * NC + lax.axis_index("c")) * NZ + lax.axis_index("z")) * NY
    number += lax.axis_index("y")
    padded = jnp.concatenate([jnp.full((DOC_MAX,), -1, jnp.int32), doc_ids], axis=0)
    key_docs = lax.dynamic_slice_in_dim(padded, number * TOK, SPAN, 0)
    routes = jnp.concatenate([expert_ids.astype(jnp.float32), route_weights], axis=1).T
    return layer(
        queries,
        keyvals.transpose(1, 0, 2),
        key_docs[None, :],
        key_docs[DOC_MAX:, None],
        routes,
        residual,
        norm_gain[None],
        out_weight,
        expert_in,
        expert_out,
    )


def solution(mesh):
    torus = Mesh(mesh.devices.reshape(NZ, NY, NX, NC), ("z", "y", "x", "c"))
    tokens = ("x", "c", "z", "y")
    experts = ("z", "y", "x", "c")
    placed = (
        P(tokens, None),
        P(tokens, None, None),
        P(tokens, None),
        P(("x", "c"), None),
        P(),
        P(),
        P(tokens, None),
        P(tokens, None),
        P(experts, None, None),
        P(experts, None, None),
    )
    return jax.shard_map(
        on_device, mesh=torus, in_specs=placed, out_specs=P(tokens, None), check_vma=False
    )
```

time: 258 us -> 221 us (0.86)
  Pallas kernels: 240 us -> 211 us
  local copies, waits for them, and re-layouts: 10.3 us -> 6.43 us
  other arithmetic: 5.35 us -> 1.97 us
    pallas_call x2 -> x1, Pallas kernels: 240 us -> 211 us  [layer(): pl.pallas_call(layer_kernel, out_shape=jax.ShapeDtypeStruct(residual.shap...]
    unnamed x14 -> x2, local copies, waits for them, and re-layouts: 9.16 us -> 3.56 us
where the time goes in v3:
time: 221 us; the launch traced here: 220 us
  Pallas kernels  211 us (95%)
  local copies, waits for them, and re-layouts  6.43 us (3%)
    pallas_call x1, Pallas kernels, layer(): pl.pallas_call(layer_kernel, out_shape=jax.ShapeDtypeStruct(residual.shap...  211 us

profile of v3, /device:TPU:2, one launch (start us, length us, event | category | flops | bytes accessed | tf_op | source)
XLA Modules:
  0.0 219.9 jit_solution(9686202535793285581)
XLA Ops:
  0.0 0.8 fusion
  0.8 0.7 convert_element_type.3
  1.4 1.3 maximum_bitcast_fusion.routes_ref
  2.7 0.8 pad_dynamic-slice_fusion.1
  3.5 0.6 broadcast_in_dim.10.key_docs_ref
  4.1 0.7 copy.12.query_docs_ref
  4.8 1.7 copy.14
  6.5 211.5 %layer.1 = bf16[128,2048]{1,0:T(8,128)(2,1)} custom-call(bf16[128,4096]{1,0:T(8,128)(2,1)} %queries_hbm.1, bf16[4,128,256]{2,1,0:T(8,128)(2,1)} %bitcast.8, s32[1,1152]{1,0:T(1,128)} %broadcast_in_dim.10.key_docs_ref, s32[128,1]{1,0:T(8,128)} %copy.12.query_docs_ref, f32[16,128]{1,0:T(8,128)} %maximum_bitcast_fusion.routes_ref, ...), custom_call_target="tpu_custom_call" | custom-call | flops 14000000000 | bytes 20971520 | tf_op jit(solution)/shard_map/layer/pallas_call | solution.py:580
  218.0 1.9 copy.16

commit v4 on v3

--- a/solution.py
+++ b/solution.py
@@ -38,6 +38,9 @@
     queries,
     residual,
     bias,
+    bias_middle,
+    bias_outer,
+    stats,
     window,
     attended,
     arrived,
@@ -198,6 +201,16 @@
     allowed = (key_docs_ref[...] == query_docs_ref[...]) & (keys_at <= tokens_at)
     bias[...] = jnp.where(allowed, 0.0, -1e30)
 
+    middle = pl.ds(pl.multiple_of((NY - y) * TOK, TOK), NY * TOK)
+    bias_middle[...] = bias[:, middle]
+
+    def outer_block(b):
+        return b + NY * ((y + b) // NY)
+
+    for b in range(NY + 1):
+        at = pl.ds(pl.multiple_of(outer_block(b) * TOK, TOK), TOK)
+        bias_outer[:, b * TOK : (b + 1) * TOK] = bias[:, at]
+
     def third(n, carry):
         g = rotated(n)
         hop(g, 2).wait_recv()
@@ -256,10 +269,49 @@
         lax.fori_loop(0, model // step, part, 0)
         share_copy(n).start()
 
+    def two_queries(g, i):
+        first_column = g * GROUP * HD + i * HD
+        return jnp.concatenate(
+            [queries[:, pl.ds(pl.multiple_of(first_column + k * HD, HD), HD)] for k in range(2)],
+            axis=0,
+        )
+
+    def score(q, keys, added):
+        scores = lax.dot_general(
+            q, keys, (((1,), (1,)), ((), ())), preferred_element_type=jnp.float32
+        )
+        return scores.reshape(2, TOK, keys.shape[0]) * scale + added
+
+    def weighted(exponent, values):
+        rows = exponent.astype(jnp.bfloat16).reshape(2 * TOK, values.shape[0])
+        total = jnp.dot(rows, values, preferred_element_type=jnp.float32)
+        return total.reshape(2, TOK, HD)
+
+    low_lanes = lax.broadcasted_iota(jnp.int32, (TOK, HD), 1) < HD // 2
+
+    def middle_part(n, carry):
+        g = rotated(n)
+        for d in range(1, NY):
+            to_row(g, 1, d).wait_recv()
+        block = window[g, NY : 2 * NY].reshape(NY * TOK, 2 * HD)
+        keys, values = block[:, :HD], block[:, HD:]
+        for i in range(0, GROUP, 2):
+            scores = score(two_queries(g, i), keys, bias_middle[...])
+            top = jnp.max(scores, axis=-1, keepdims=True)
+            exponent = jnp.exp2(scores - top)
+            denominator = jnp.sum(exponent, axis=-1, keepdims=True)
+            numerator = weighted(exponent, values)
+            for k in range(2):
+                rows = pl.ds(pl.multiple_of(lax.rem(g, 2) * TOK, TOK), TOK)
+                home[g // 2, rows, (i + k) * HD : (i + k + 1) * HD] = numerator[k]
+                stats[g, i + k] = jnp.where(low_lanes, top[k], denominator[k])
+        return carry
+
+    lax.fori_loop(0, KVH, middle_part, 0)
+
     def one_kv_head(n, carry):
         g = rotated(n)
         for d in range(1, NY):
-            to_row(g, 1, d).wait_recv()
 
             @pl.when(y >= d)
             def _():
@@ -269,29 +321,21 @@
             def _():
                 to_row(g, 0, d).wait_recv()
 
-        keys = window[g, pl.ds(y, SPAN // TOK), :, 0:HD].reshape(SPAN, HD)
-        values = window[g, pl.ds(y, SPAN // TOK), :, HD:].reshape(SPAN, HD)
+        blocks = [window[g, y + outer_block(b)] for b in range(NY + 1)]
+        keys = jnp.concatenate([block[:, :HD] for block in blocks], axis=0)
+        values = jnp.concatenate([block[:, HD:] for block in blocks], axis=0)
         for i in range(0, GROUP, 2):
-            first_column = g * GROUP * HD + i * HD
-            q = [
-                queries[:, pl.ds(pl.multiple_of(first_column + k * HD, HD), HD)] for k in range(2)
-            ]
-            scores = lax.dot_general(
-                jnp.concatenate(q, axis=0),
-                keys,
-                (((1,), (1,)), ((), ())),
-                preferred_element_type=jnp.float32,
-            )
-            scores = scores.reshape(2, TOK, SPAN) * scale + bias[...]
-            top = jnp.max(scores, axis=-1, keepdims=True)
+            scores = score(two_queries(g, i), keys, bias_outer[...])
+            rows = pl.ds(pl.multiple_of(lax.rem(g, 2) * TOK, TOK), TOK)
+            before = [home[g // 2, rows, (i + k) * HD : (i + k + 1) * HD] for k in range(2)]
+            before_top = jnp.stack([stats[g, i + k][:, :1] for k in range(2)])
+            before_sum = jnp.stack([stats[g, i + k][:, HD // 2 : HD // 2 + 1] for k in range(2)])
+            top = jnp.maximum(jnp.max(scores, axis=-1, keepdims=True), before_top)
             exponent = jnp.exp2(scores - top)
-            denominator = jnp.sum(exponent, axis=-1, keepdims=True)
-            numerator = jnp.dot(
-                exponent.astype(jnp.bfloat16).reshape(2 * TOK, SPAN),
-                values,
-                preferred_element_type=jnp.float32,
-            )
-            result = (numerator.reshape(2, TOK, HD) / denominator).astype(jnp.bfloat16)
+            factor = jnp.exp2(before_top - top)
+            denominator = jnp.sum(exponent, axis=-1, keepdims=True) + factor * before_sum
+            numerator = weighted(exponent, values) + factor * jnp.stack(before)
+            result = (numerator / denominator).astype(jnp.bfloat16)
             for k in range(2):
                 attended[g, :, (i + k) * HD : (i + k + 1) * HD] = result[k]
 
@@ -586,6 +630,9 @@
             pltpu.VMEM(queries.shape, bf16),
             pltpu.VMEM(residual.shape, bf16),
             pltpu.VMEM((TOK, SPAN), f32),
+            pltpu.VMEM((TOK, NY * TOK), f32),
+            pltpu.VMEM((TOK, (NY + 1) * TOK), f32),
+            pltpu.VMEM((KVH, GROUP, TOK, HD), f32),
             pltpu.VMEM((KVH, 3 * NY, TOK, 2 * HD), bf16),
             pltpu.VMEM((KVH, TOK, half), bf16),
             pltpu.VMEM((NX, TOK, half), bf16),

time: 221 us -> 210 us (0.950)
  the two profiles are of different devices: /device:TPU:2 before, /device:TPU:16 now
where the time goes in v4:
time: 210 us; the launch traced here: 209 us
  Pallas kernels  201 us (96%)
  local copies, waits for them, and re-layouts  6.42 us (3%)
    pallas_call x1, Pallas kernels, layer(): pl.pallas_call(layer_kernel, out_shape=jax.ShapeDtypeStruct(residual.shap...  201 us

profile of v4, /device:TPU:16, one launch (start us, length us, event | category | flops | bytes accessed | tf_op | source)
XLA Modules:
  0.0 209.4 jit_solution(2685047640068469410)
XLA Ops:
  0.0 0.8 fusion
  0.8 0.7 convert_element_type.3
  1.4 1.3 maximum_bitcast_fusion.routes_ref
  2.7 0.8 pad_dynamic-slice_fusion.1
  3.5 0.6 broadcast_in_dim.10.key_docs_ref
  4.1 0.7 copy.12.query_docs_ref
  4.8 1.7 copy.14
  6.5 201.0 %layer.1 = bf16[128,2048]{1,0:T(8,128)(2,1)} custom-call(bf16[128,4096]{1,0:T(8,128)(2,1)} %queries_hbm.1, bf16[4,128,256]{2,1,0:T(8,128)(2,1)} %bitcast.8, s32[1,1152]{1,0:T(1,128)} %broadcast_in_dim.10.key_docs_ref, s32[128,1]{1,0:T(8,128)} %copy.12.query_docs_ref, f32[16,128]{1,0:T(8,128)} %maximum_bitcast_fusion.routes_ref, ...), custom_call_target="tpu_custom_call" | custom-call | flops 14000000000 | bytes 20971520 | tf_op jit(solution)/shard_map/layer/pallas_call | solution.py:624
  207.5 1.9 copy.16

commit v5 on v4

--- a/solution.py
+++ b/solution.py
@@ -516,7 +516,6 @@
             for copy in weight_copies:
                 copy.wait()
         expert(groups[n - 1])
-    expert(groups[4])
 
     def give_back(n):
         for r in groups[n]:
@@ -551,8 +550,9 @@
 
         lax.fori_loop(0, wide // step, part, 0)
 
+    give_back(3)
+    expert(groups[4])
     give_back(4)
-    give_back(3)
     for n in (4, 3, 2, 1, 0):
         for k, r in enumerate(groups[n]):
             whole(recv, back, back_send, back_recv, r).wait_recv()

time: 210 us -> 208 us (level)
  the two profiles are of different devices: /device:TPU:16 before, /device:TPU:2 now
where the time goes in v5:
time: 208 us; the launch traced here: 207 us
  Pallas kernels  199 us (96%)
  local copies, waits for them, and re-layouts  6.43 us (3%)
    pallas_call x1, Pallas kernels, layer(): pl.pallas_call(layer_kernel, out_shape=jax.ShapeDtypeStruct(residual.shap...  199 us

profile of v5, /device:TPU:2, one launch (start us, length us, event | category | flops | bytes accessed | tf_op | source)
XLA Modules:
  0.0 207.5 jit_solution(9559161085138075926)
XLA Ops:
  0.0 0.8 fusion
  0.8 0.7 convert_element_type.3
  1.4 1.3 maximum_bitcast_fusion.routes_ref
  2.7 0.8 pad_dynamic-slice_fusion.1
  3.5 0.6 broadcast_in_dim.10.key_docs_ref
  4.1 0.7 copy.12.query_docs_ref
  4.8 1.7 copy.14
  6.5 199.0 %layer.1 = bf16[128,2048]{1,0:T(8,128)(2,1)} custom-call(bf16[128,4096]{1,0:T(8,128)(2,1)} %queries_hbm.1, bf16[4,128,256]{2,1,0:T(8,128)(2,1)} %bitcast.8, s32[1,1152]{1,0:T(1,128)} %broadcast_in_dim.10.key_docs_ref, s32[128,1]{1,0:T(8,128)} %copy.12.query_docs_ref, f32[16,128]{1,0:T(8,128)} %maximum_bitcast_fusion.routes_ref, ...), custom_call_target="tpu_custom_call" | custom-call | flops 14000000000 | bytes 20971520 | tf_op jit(solution)/shard_map/layer/pallas_call | solution.py:624
  205.6 1.9 copy.16
